TPU v7x, 32 devices: a whole 2x2x4 slice. The times are simulated.
32 devices in a mesh: kpt: 2 (over y), dom: 8 (over z, x), band: 2 (over core).
Axes of the slice: x: 2, y: 2, z: 4, core: 2. Of those that a mesh axis runs over, the one named last changes fastest.
Arguments:
- wavefunctions: bfloat16 [65536, 256], P(('kpt', 'dom'), 'band'), parts along dimension 0, may hold values from -40 to 40
- bounds: float32 [4], P('kpt'), parts along dimension 0, may hold values from 0.5 to 23, as said below
- cell_matrix: bfloat16 [512, 512], replicated, may hold values from -1 to 4, as said below
- cell_scale: float32 [128], P('dom'), may hold values from 0.5 to 6
- potential: float32 [32768], P('dom'), may hold values from 0.5 to 3
- cell_nodes: int32 [128, 512], P('dom'), may hold values from 0 to 5119, as said below
- face_nodes: int32 [32, 256], P('dom'), may hold values from -1 to 4095, as said below
Outputs:
- rotated: float32 [65536, 256], P(('kpt', 'dom'), 'band'), parts along dimension 0
There are 2 independent parts, one for each index of `kpt`. A program takes and returns all parts, laid end to end along the dimension named above; an argument that names none is the same for every part. Nothing has to cross between parts.
Inputs may be any that keep to these rules, and one draw needn't show every extreme that they name: `face_nodes`: row 4 d + o lists in its first slots the own nodes (0 to 4095 of block d) sent to block d + (1, -1, 2, -2)[o]; the remaining slots hold -1; at least one row whose neighbour block exists is full. `cell_nodes`: entries below 4096 are own nodes of the cell's block, the others ghost rows of its extended block. bounds[1] exceeds bounds[0] by 8 or more. `cell_matrix`: symmetric.
All inputs are finite; a program needn't handle non-finite values.
Results may differ from a plain program's by a relative error of at most 0.0054.
Values may be sent and summed in bfloat16 or wider, within the bound.
A program may use at most 64 MiB of HBM per device.

v0:
```python
import jax
import jax.numpy as jnp
from jax import lax
from jax.sharding import PartitionSpec as P

peer_offsets = (1, -1, 2, -2)


def passed_along(value, axis, by):
    size = lax.axis_size(axis)
    pairs = [(i, i + by) for i in range(size) if 0 <= i + by < size]
    return lax.ppermute(value, axis, pairs)


def on_device(wavefunctions, bounds, cell_matrix, cell_scale, potential, cell_nodes, face_nodes):
    node_dev, columns = wavefunctions.shape
    slot_count = face_nodes.shape[1]
    ext_count = node_dev + 4 * slot_count
    filled = face_nodes >= 0
    safe_index = jnp.maximum(face_nodes, 0)
    targets = jnp.where(filled, face_nodes, node_dev).reshape(-1)
    flat_maps = cell_nodes.reshape(-1)

    def apply_operator(vectors):
        outgoing = jnp.where(filled[:, :, None], vectors[safe_index], jnp.zeros((), vectors.dtype))
        ghosts = [None, None, None, None]
        for offset_idx in range(4):
            ghosts[offset_idx] = passed_along(outgoing[offset_idx], "dom", peer_offsets[offset_idx])
        extended = jnp.concatenate([vectors] + ghosts, 0)
        gathered = extended[cell_nodes]
        products = jnp.einsum(
            "ij,cjk->cik", cell_matrix, gathered, preferred_element_type=jnp.float32
        )
        products = products * cell_scale[:, None, None]
        summed = jax.ops.segment_sum(
            products.reshape(-1, columns), flat_maps, num_segments=ext_count
        )
        ghost_acc = summed[node_dev:].reshape(4, slot_count, columns)
        returned = [None, None, None, None]
        for offset_idx in range(4):
            returned[offset_idx] = passed_along(
                ghost_acc[offset_idx], "dom", -peer_offsets[offset_idx]
            )
        returned_sum = jax.ops.segment_sum(
            jnp.stack(returned).reshape(-1, columns), targets, num_segments=node_dev + 1
        )
        return (
            summed[:node_dev]
            + returned_sum[:node_dev]
            + potential[:, None] * vectors.astype(jnp.float32)
        )

    center = (bounds[0] + bounds[1]) / 2.0
    half_width = (bounds[1] - bounds[0]) / 2.0
    wave_wide = wavefunctions.astype(jnp.float32)
    image_one = apply_operator(wavefunctions)
    degree_one = ((image_one - center * wave_wide) / half_width).astype(jnp.bfloat16)
    image_two = apply_operator(degree_one)
    degree_two = (
        2.0 * (image_two - center * degree_one.astype(jnp.float32)) / half_width - wave_wide
    ).astype(jnp.bfloat16)
    panel_all = lax.all_gather(degree_two, "band", axis=1, tiled=True)
    band_count = panel_all.shape[1]
    node_count = node_dev * lax.axis_size("dom")
    col_start = lax.axis_index("band") * columns
    margin_part = jnp.einsum("nc,nd->cd", degree_two, panel_all, preferred_element_type=jnp.float32)
    margin_part = lax.psum(margin_part, "dom")
    margin = lax.all_gather(margin_part, "band", axis=0, tiled=True)
    margin = margin / node_count
    factor = jnp.linalg.cholesky(margin)
    inverse = lax.linalg.triangular_solve(
        factor, jnp.eye(band_count, dtype=factor.dtype), left_side=True, lower=True
    )
    own_rows = lax.dynamic_slice_in_dim(inverse, col_start, columns, 0)
    return jnp.dot(panel_all.astype(jnp.float32), own_rows.T, precision=lax.Precision.HIGHEST)


def solution(mesh):
    return jax.shard_map(
        on_device,
        mesh=mesh,
        in_specs=(
            P(("kpt", "dom"), "band"),
            P("kpt"),
            P(),
            P("dom"),
            P("dom"),
            P("dom", None),
            P("dom", None),
        ),
        out_specs=P(("kpt", "dom"), "band"),
        check_vma=False,
    )
```

profile of v0, /device:TPU:0, one launch (start us, length us, event | category | flops | bytes accessed | tf_op | source)
XLA Modules:
  0.0 440.5 jit_solution(5676288269677081462)
XLA Ops:
  8.1 4.2 gather_fusion
  12.5 4.8 %collective-permute-start = (bf16[256,128]{1,0:T(8,128)(2,1)S(1)}, bf16[256,128]{1,0:T(8,128)(2,1)S(1)}, u32[]{:S(2)}, u32[]{:S(2)}) collective-permute-start(bf16[256,128]{1,0:T(8,128)(2,1)S(1)} %get-tuple-element.40), channel_id=1, source_target_pairs={{0,2},{2,4},{4,6},{6,8},{8,10},{10,12},{12,14},{1,3},{3,5},{5,7},{... | collective-permute-start | bytes 196616 | tf_op jit(solution)/shard_map/ppermute | solution.py:12
  17.4 1.3 collective-permute-start.1
  18.7 5.5 %collective-permute-start.2 = (bf16[256,128]{1,0:T(8,128)(2,1)S(1)}, bf16[256,128]{1,0:T(8,128)(2,1)S(1)}, u32[]{:S(2)}, u32[]{:S(2)}) collective-permute-start(bf16[256,128]{1,0:T(8,128)(2,1)S(1)} %get-tuple-element.38), channel_id=1, source_target_pairs={{0,4},{2,6},{4,8},{6,10},{8,12},{10,14},{1,5},{3,7},{5,9},{7,11},{... | collective-permute-start | bytes 196616 | tf_op jit(solution)/shard_map/ppermute | solution.py:12
  24.2 1.3 collective-permute-start.3
  26.1 4.3 collective-permute-done.3
  30.4 29.5 %gather_fusion.1 = bf16[8192,128]{1,0:T(8,128)(2,1)} fusion(bf16[5120,128]{1,0:T(8,128)(2,1)S(1)} %constant_dynamic-update-slice_fusion, s32[8192]{0:T(1024)S(1)} %broadcast_clamp_fusion), kind=kCustom, calls=%fused_computation.1 | custom fusion | bytes 4227072 | tf_op jit(solution)/shard_map/gather | solution.py:30
  59.9 5.2 %multiply_bitcast_fusion.1 = f32[16,512,128]{1,2,0:T(8,128)} fusion(bf16[16,512,128]{2,1,0:T(8,128)(2,1)} %bitcast.91, f32[16]{0:T(128)S(1)} %copy-done.6, bf16[512,512]{1,0:T(8,128)(2,1)S(1)} %copy-done), kind=kOutput, calls=%fused_computation.11 | convolution fusion | flops 1074790400 | bytes 6815808 | tf_op jit(solution)/shard_map/ij,cjk->cik/dot_general | solution.py:31
  65.2 5.4 %copy.13 = f32[16,512,128]{2,1,0:T(8,128)} copy(f32[16,512,128]{1,2,0:T(8,128)} %multiply_bitcast_fusion.1) | data formatting | bytes 8388608 | tf_op jit(solution)/shard_map/mul | solution.py:34
  70.5 46.0 %scatter_custom_fusion = f32[5120,128]{1,0:T(8,128)} fusion(s32[8192]{0:T(1024)S(1)} %bitcast.108, f32[8192,128]{1,0:T(8,128)} %bitcast.93, f32[]{:T(128)} %constant.94.clone.1), kind=kCustom, calls=%fused_computation.30 | custom fusion | flops 1048576 | bytes 2621952 | tf_op jit(solution)/shard_map/scatter-add | solution.py:35
  116.5 1.1 fusion.36
  117.6 2.5 collective-permute-start.5
  120.1 1.3 collective-permute-start.6
  121.4 4.6 %collective-permute-start.7 = (f32[256,128]{1,0:T(8,128)S(1)}, f32[256,128]{1,0:T(8,128)S(1)}, u32[]{:S(2)}, u32[]{:S(2)}) collective-permute-start(f32[256,128]{1,0:T(8,128)S(1)} %get-tuple-element.30), channel_id=1, source_target_pairs={{0,4},{2,6},{4,8},{6,10},{8,12},{10,14},{1,5},{3,7},{5,9},{7,11},{... | collective-permute-start | bytes 393224 | tf_op jit(solution)/shard_map/ppermute | solution.py:12
  126.0 1.3 collective-permute-start.4
  130.5 2.8 collective-permute-done.4
  133.3 8.2 %scatter_custom_fusion.1 = f32[4097,128]{1,0:T(8,128)} fusion(s32[1024]{0:T(1024)S(1)} %bitcast.111, f32[1024,128]{1,0:T(8,128)S(1)} %bitcast.97, f32[]{:T(128)} %constant.94.clone.1), kind=kCustom, calls=%fused_computation.36 | custom fusion | flops 131072 | bytes 2097668 | tf_op jit(solution)/shard_map/scatter-add | solution.py:44
  141.5 3.3 constant_dynamic-update-slice_fusion.9
  144.8 4.2 gather_fusion.2
  149.3 4.9 %collective-permute-start.8 = (bf16[256,128]{1,0:T(8,128)(2,1)S(1)}, bf16[256,128]{1,0:T(8,128)(2,1)S(1)}, u32[]{:S(2)}, u32[]{:S(2)}) collective-permute-start(bf16[256,128]{1,0:T(8,128)(2,1)S(1)} %get-tuple-element.36), channel_id=1, source_target_pairs={{0,2},{2,4},{4,6},{6,8},{8,10},{10,12},{12,14},{1,3},{3,5},{5,7},{... | collective-permute-start | bytes 196616 | tf_op jit(solution)/shard_map/ppermute | solution.py:12
  154.2 1.3 collective-permute-start.9
  155.5 4.0 collective-permute-start.10
  159.5 1.5 collective-permute-start.11
  161.4 4.3 collective-permute-done.11
  165.7 29.5 %gather_fusion.3 = bf16[8192,128]{1,0:T(8,128)(2,1)} fusion(bf16[5120,128]{1,0:T(8,128)(2,1)S(1)} %constant_dynamic-update-slice_fusion.5, s32[8192]{0:T(1024)S(1)} %broadcast_clamp_fusion), kind=kCustom, calls=%fused_computation.3 | custom fusion | bytes 4227072 | tf_op jit(solution)/shard_map/gather | solution.py:30
  195.2 5.2 %multiply_bitcast_fusion = f32[16,512,128]{1,2,0:T(8,128)} fusion(bf16[16,512,128]{2,1,0:T(8,128)(2,1)} %bitcast.90, f32[16]{0:T(128)S(1)} %copy-done.6, bf16[512,512]{1,0:T(8,128)(2,1)S(1)} %copy-done), kind=kOutput, calls=%fused_computation.10 | convolution fusion | flops 1074790400 | bytes 6815808 | tf_op jit(solution)/shard_map/ij,cjk->cik/dot_general | solution.py:31
  200.4 5.4 %copy.15 = f32[16,512,128]{2,1,0:T(8,128)} copy(f32[16,512,128]{1,2,0:T(8,128)} %multiply_bitcast_fusion) | data formatting | bytes 8388608 | tf_op jit(solution)/shard_map/mul | solution.py:34
  205.8 46.0 %scatter_custom_fusion.2 = f32[5120,128]{1,0:T(8,128)} fusion(s32[8192]{0:T(1024)S(1)} %bitcast.109, f32[8192,128]{1,0:T(8,128)} %bitcast.92, f32[]{:T(128)} %constant.94.clone.1), kind=kCustom, calls=%fused_computation.28 | custom fusion | flops 1048576 | bytes 2621952 | tf_op jit(solution)/shard_map/scatter-add | solution.py:35
  251.7 1.2 fusion.35
  253.0 1.3 collective-permute-start.12
  254.3 4.6 %collective-permute-start.13 = (f32[256,128]{1,0:T(8,128)S(1)}, f32[256,128]{1,0:T(8,128)S(1)}, u32[]{:S(2)}, u32[]{:S(2)}) collective-permute-start(f32[256,128]{1,0:T(8,128)S(1)} %get-tuple-element.28), channel_id=1, source_target_pairs={{0,2},{2,4},{4,6},{6,8},{8,10},{10,12},{12,14},{1,3},{3,5},{5,7},{... | collective-permute-start | bytes 393224 | tf_op jit(solution)/shard_map/ppermute | solution.py:12
  258.8 1.3 collective-permute-start.14
  260.1 4.6 %collective-permute-start.15 = (f32[256,128]{1,0:T(8,128)S(1)}, f32[256,128]{1,0:T(8,128)S(1)}, u32[]{:S(2)}, u32[]{:S(2)}) collective-permute-start(f32[256,128]{1,0:T(8,128)S(1)} %get-tuple-element.26), channel_id=1, source_target_pairs={{0,4},{2,6},{4,8},{6,10},{8,12},{10,14},{1,5},{3,7},{5,9},{7,11},{... | collective-permute-start | bytes 393224 | tf_op jit(solution)/shard_map/ppermute | solution.py:12
  265.7 1.5 collective-permute-done.15
  267.2 8.2 %scatter_custom_fusion.3 = f32[4097,128]{1,0:T(8,128)} fusion(s32[1024]{0:T(1024)S(1)} %bitcast.112, f32[1024,128]{1,0:T(8,128)S(1)} %bitcast.96, f32[]{:T(128)} %constant.94.clone.1), kind=kCustom, calls=%fused_computation.34 | custom fusion | flops 131072 | bytes 2097668 | tf_op jit(solution)/shard_map/scatter-add | solution.py:44
  275.4 3.4 fusion.8
  278.9 11.5 %all-gather.2.cloned.1.call-done = bf16[4096,256]{1,0:T(8,128)(2,1)} async-done(((bf16[4096,128]{1,0:T(8,128)(2,1)}), bf16[4096,256]{1,0:T(8,128)(2,1)}) %all-gather.2.cloned.1.call-update) | async-done | bytes 2097168 | tf_op jit(solution)/shard_map/all_gather | solution.py:62
  290.3 3.5 fusion.38
  293.9 71.0 %all-reduce.3.cloned.1.call-done = f32[128,256]{0,1:T(8,128)} async-done(((f32[128,256]{0,1:T(8,128)}), f32[128,256]{0,1:T(8,128)}) %all-reduce.3.cloned.1.call-update) | async-done | bytes 131088 | tf_op jit(solution)/shard_map/psum | solution.py:67
  365.0 2.5 all_gather.7
  367.7 11.7 %cholesky.50 = f32[128,128]{1,0:T(8,128)S(1)} custom-call(f32[128,128]{1,0:T(8,128)S(1)} %cholesky.118), custom_call_target="Cholesky" | custom-call | tf_op jit(solution)/shard_map/jit(cholesky)/cholesky | solution.py:70
  379.5 9.8 %custom-call.14 = f32[1,128,128]{1,2,0:T(8,128)S(1)} custom-call(f32[1,128,128]{2,1,0:T(8,128)S(1)} %get-tuple-element.44), custom_call_target="InvertDiagBlocksLowerTriangular" | custom-call | tf_op jit(solution)/shard_map/jit(cholesky)/cholesky | solution.py:70
  389.8 11.7 %cholesky.105 = f32[128,128]{1,0:T(8,128)S(1)} custom-call(f32[128,128]{1,0:T(8,128)S(1)} %convolution_subtract_fusion.1), custom_call_target="Cholesky" | custom-call | tf_op jit(solution)/shard_map/jit(cholesky)/cholesky | solution.py:70
  403.7 5.5 %while.1 = (s32[]{:T(128)}, f32[256,256]{1,0:T(8,128)S(1)}, s32[2,2]{1,0:T(2,128)S(1)}, f32[2,128,128]{2,1,0:T(8,128)}, s32[]{:T(128)}) while((s32[]{:T(128)}, f32[256,256]{1,0:T(8,128)S(1)}, s32[2,2]{1,0:T(2,128)S(1)}, f32[2,128,128]{2,1,0:T(8,128)}, s32[]{:T(128)}) %tuple.38), condition=%wide.while_cond, body=%wide.while_body.sunk | while | flops 2 | bytes 132705 | solution.py:71
  404.5 2.0 bitcast_dynamic-update-slice_fusion.2
  407.1 2.0 bitcast_dynamic-update-slice_fusion.2
  409.2 20.5 %custom-call.15 = f32[2,128,128]{1,2,0:T(8,128)S(1)} custom-call(f32[2,128,128]{2,1,0:T(8,128)} %get-tuple-element.12), custom_call_target="InvertDiagBlocksLowerTriangular" | custom-call | tf_op jit(solution)/shard_map/triangular_solve | solution.py:71
  430.5 3.2 fusion.21
  (79 shorter events, 8.3 us)
Async XLA Ops:
  6.5 53.4 %copy-start = (bf16[512,512]{1,0:T(8,128)(2,1)S(1)}, bf16[512,512]{1,0:T(8,128)(2,1)}, u32[]{:S(2)}) copy-start(bf16[512,512]{1,0:T(8,128)(2,1)} %param.9) | copy-start | bytes 1572868
  6.5 19.0 %copy-start.1 = (bf16[4096,128]{1,0:T(8,128)(2,1)S(1)}, bf16[4096,128]{1,0:T(8,128)(2,1)}, u32[]{:S(2)}) copy-start(bf16[4096,128]{1,0:T(8,128)(2,1)} %param.7) | copy-start | bytes 3145732
  6.5 283.8 %all-gather.2.cloned.1.call-start = ((), (), s32[]{:S(2)}) async-start(), calls=%async_computation | async-start | bytes 3145728 | tf_op jit(solution)/shard_map/all_gather | solution.py:62
  12.3 13.3 %copy-start.4 = (s32[16,512]{1,0:T(8,128)S(1)}, s32[16,512]{1,0:T(8,128)}, u32[]{:S(2)}) copy-start(s32[16,512]{1,0:T(8,128)} %param.12) | copy-start | bytes 98308
  12.5 13.2 %collective-permute-start = (bf16[256,128]{1,0:T(8,128)(2,1)S(1)}, bf16[256,128]{1,0:T(8,128)(2,1)S(1)}, u32[]{:S(2)}, u32[]{:S(2)}) collective-permute-start(bf16[256,128]{1,0:T(8,128)(2,1)S(1)} %get-tuple-element.40), channel_id=1, source_target_pairs={{0,2},{2,4},{4,6},{6,8},{8,10},{10,12},{12,14},{1,3},{3,5},{5,7},{... | collective-permute-start | bytes 196616 | tf_op jit(solution)/shard_map/ppermute | solution.py:12
  17.4 8.3 %collective-permute-start.1 = (bf16[256,128]{1,0:T(8,128)(2,1)S(1)}, bf16[256,128]{1,0:T(8,128)(2,1)S(1)}, u32[]{:S(2)}, u32[]{:S(2)}) collective-permute-start(bf16[256,128]{1,0:T(8,128)(2,1)S(1)} %get-tuple-element.39), channel_id=1, source_target_pairs={{2,0},{4,2},{6,4},{8,6},{10,8},{12,10},{14,12},{3,1},{5,3},{7,5},{... | collective-permute-start | bytes 196616 | tf_op jit(solution)/shard_map/ppermute | solution.py:12
  18.7 7.4 %collective-permute-start.2 = (bf16[256,128]{1,0:T(8,128)(2,1)S(1)}, bf16[256,128]{1,0:T(8,128)(2,1)S(1)}, u32[]{:S(2)}, u32[]{:S(2)}) collective-permute-start(bf16[256,128]{1,0:T(8,128)(2,1)S(1)} %get-tuple-element.38), channel_id=1, source_target_pairs={{0,4},{2,6},{4,8},{6,10},{8,12},{10,14},{1,5},{3,7},{5,9},{7,11},{... | collective-permute-start | bytes 196616 | tf_op jit(solution)/shard_map/ppermute | solution.py:12
  24.2 6.2 %collective-permute-start.3 = (bf16[256,128]{1,0:T(8,128)(2,1)S(1)}, bf16[256,128]{1,0:T(8,128)(2,1)S(1)}, u32[]{:S(2)}, u32[]{:S(2)}) collective-permute-start(bf16[256,128]{1,0:T(8,128)(2,1)S(1)} %get-tuple-element.37), channel_id=1, source_target_pairs={{4,0},{6,2},{8,4},{10,6},{12,8},{14,10},{5,1},{7,3},{9,5},{11,7},{... | collective-permute-start | bytes 196616 | tf_op jit(solution)/shard_map/ppermute | solution.py:12
  30.4 29.5 %copy-start.6 = (f32[16]{0:T(128)S(1)}, f32[16]{0:T(128)}, u32[]{:S(2)}) copy-start(f32[16]{0:T(128)} %param.10) | copy-start | bytes 196
  70.5 56.8 %copy-start.7 = (f32[2]{0:T(128)S(1)}, f32[2]{0:T(128)}, u32[]{:S(2)}) copy-start(f32[2]{0:T(128)} %param.8) | copy-start | bytes 28
  116.5 25.0 %copy-start.5 = (f32[4096]{0:T(1024)S(1)}, f32[4096]{0:T(1024)}, u32[]{:S(2)}) copy-start(f32[4096]{0:T(1024)} %param.11) | copy-start | bytes 49156
  117.6 12.9 %collective-permute-start.5 = (f32[256,128]{1,0:T(8,128)S(1)}, f32[256,128]{1,0:T(8,128)S(1)}, u32[]{:S(2)}, u32[]{:S(2)}) collective-permute-start(f32[256,128]{1,0:T(8,128)S(1)} %get-tuple-element.32), channel_id=1, source_target_pairs={{0,2},{2,4},{4,6},{6,8},{8,10},{10,12},{12,14},{1,3},{3,5},{5,7},{... | collective-permute-start | bytes 393224 | tf_op jit(solution)/shard_map/ppermute | solution.py:12
  120.1 10.4 %collective-permute-start.6 = (f32[256,128]{1,0:T(8,128)S(1)}, f32[256,128]{1,0:T(8,128)S(1)}, u32[]{:S(2)}, u32[]{:S(2)}) collective-permute-start(f32[256,128]{1,0:T(8,128)S(1)} %get-tuple-element.31), channel_id=1, source_target_pairs={{4,0},{6,2},{8,4},{10,6},{12,8},{14,10},{5,1},{7,3},{9,5},{11,7},{... | collective-permute-start | bytes 393224 | tf_op jit(solution)/shard_map/ppermute | solution.py:12
  121.4 9.1 %collective-permute-start.7 = (f32[256,128]{1,0:T(8,128)S(1)}, f32[256,128]{1,0:T(8,128)S(1)}, u32[]{:S(2)}, u32[]{:S(2)}) collective-permute-start(f32[256,128]{1,0:T(8,128)S(1)} %get-tuple-element.30), channel_id=1, source_target_pairs={{0,4},{2,6},{4,8},{6,10},{8,12},{10,14},{1,5},{3,7},{5,9},{7,11},{... | collective-permute-start | bytes 393224 | tf_op jit(solution)/shard_map/ppermute | solution.py:12
  126.0 7.3 %collective-permute-start.4 = (f32[256,128]{1,0:T(8,128)S(1)}, f32[256,128]{1,0:T(8,128)S(1)}, u32[]{:S(2)}, u32[]{:S(2)}) collective-permute-start(f32[256,128]{1,0:T(8,128)S(1)} %get-tuple-element.29), channel_id=1, source_target_pairs={{2,0},{4,2},{6,4},{8,6},{10,8},{12,10},{14,12},{3,1},{5,3},{7,5},{... | collective-permute-start | bytes 393224 | tf_op jit(solution)/shard_map/ppermute | solution.py:12
  149.3 11.7 %collective-permute-start.8 = (bf16[256,128]{1,0:T(8,128)(2,1)S(1)}, bf16[256,128]{1,0:T(8,128)(2,1)S(1)}, u32[]{:S(2)}, u32[]{:S(2)}) collective-permute-start(bf16[256,128]{1,0:T(8,128)(2,1)S(1)} %get-tuple-element.36), channel_id=1, source_target_pairs={{0,2},{2,4},{4,6},{6,8},{8,10},{10,12},{12,14},{1,3},{3,5},{5,7},{... | collective-permute-start | bytes 196616 | tf_op jit(solution)/shard_map/ppermute | solution.py:12
  154.2 6.8 %collective-permute-start.9 = (bf16[256,128]{1,0:T(8,128)(2,1)S(1)}, bf16[256,128]{1,0:T(8,128)(2,1)S(1)}, u32[]{:S(2)}, u32[]{:S(2)}) collective-permute-start(bf16[256,128]{1,0:T(8,128)(2,1)S(1)} %get-tuple-element.35), channel_id=1, source_target_pairs={{2,0},{4,2},{6,4},{8,6},{10,8},{12,10},{14,12},{3,1},{5,3},{7,5},{... | collective-permute-start | bytes 196616 | tf_op jit(solution)/shard_map/ppermute | solution.py:12
  155.5 5.9 %collective-permute-start.10 = (bf16[256,128]{1,0:T(8,128)(2,1)S(1)}, bf16[256,128]{1,0:T(8,128)(2,1)S(1)}, u32[]{:S(2)}, u32[]{:S(2)}) collective-permute-start(bf16[256,128]{1,0:T(8,128)(2,1)S(1)} %get-tuple-element.34), channel_id=1, source_target_pairs={{0,4},{2,6},{4,8},{6,10},{8,12},{10,14},{1,5},{3,7},{5,9},{7,11},{... | collective-permute-start | bytes 196616 | tf_op jit(solution)/shard_map/ppermute | solution.py:12
  159.5 6.2 %collective-permute-start.11 = (bf16[256,128]{1,0:T(8,128)(2,1)S(1)}, bf16[256,128]{1,0:T(8,128)(2,1)S(1)}, u32[]{:S(2)}, u32[]{:S(2)}) collective-permute-start(bf16[256,128]{1,0:T(8,128)(2,1)S(1)} %get-tuple-element.33), channel_id=1, source_target_pairs={{4,0},{6,2},{8,4},{10,6},{12,8},{14,10},{5,1},{7,3},{9,5},{11,7},{... | collective-permute-start | bytes 196616 | tf_op jit(solution)/shard_map/ppermute | solution.py:12
  251.7 23.6 %copy-start.2 = (bf16[4096,128]{1,0:T(8,128)(2,1)S(1)}, bf16[4096,128]{1,0:T(8,128)(2,1)}, u32[]{:S(2)}) copy-start(bf16[4096,128]{1,0:T(8,128)(2,1)} %get-tuple-element.22) | copy-start | bytes 3145732
  253.0 11.7 %collective-permute-start.12 = (f32[256,128]{1,0:T(8,128)S(1)}, f32[256,128]{1,0:T(8,128)S(1)}, u32[]{:S(2)}, u32[]{:S(2)}) collective-permute-start(f32[256,128]{1,0:T(8,128)S(1)} %get-tuple-element.25), channel_id=1, source_target_pairs={{2,0},{4,2},{6,4},{8,6},{10,8},{12,10},{14,12},{3,1},{5,3},{7,5},{... | collective-permute-start | bytes 393224 | tf_op jit(solution)/shard_map/ppermute | solution.py:12
  254.3 10.4 %collective-permute-start.13 = (f32[256,128]{1,0:T(8,128)S(1)}, f32[256,128]{1,0:T(8,128)S(1)}, u32[]{:S(2)}, u32[]{:S(2)}) collective-permute-start(f32[256,128]{1,0:T(8,128)S(1)} %get-tuple-element.28), channel_id=1, source_target_pairs={{0,2},{2,4},{4,6},{6,8},{8,10},{10,12},{12,14},{1,3},{3,5},{5,7},{... | collective-permute-start | bytes 393224 | tf_op jit(solution)/shard_map/ppermute | solution.py:12
  258.8 6.9 %collective-permute-start.14 = (f32[256,128]{1,0:T(8,128)S(1)}, f32[256,128]{1,0:T(8,128)S(1)}, u32[]{:S(2)}, u32[]{:S(2)}) collective-permute-start(f32[256,128]{1,0:T(8,128)S(1)} %get-tuple-element.27), channel_id=1, source_target_pairs={{4,0},{6,2},{8,4},{10,6},{12,8},{14,10},{5,1},{7,3},{9,5},{11,7},{... | collective-permute-start | bytes 393224 | tf_op jit(solution)/shard_map/ppermute | solution.py:12
  260.1 7.1 %collective-permute-start.15 = (f32[256,128]{1,0:T(8,128)S(1)}, f32[256,128]{1,0:T(8,128)S(1)}, u32[]{:S(2)}, u32[]{:S(2)}) collective-permute-start(f32[256,128]{1,0:T(8,128)S(1)} %get-tuple-element.26), channel_id=1, source_target_pairs={{0,4},{2,6},{4,8},{6,10},{8,12},{10,14},{1,5},{3,7},{5,9},{7,11},{... | collective-permute-start | bytes 393224 | tf_op jit(solution)/shard_map/ppermute | solution.py:12
  278.8 86.1 %all-reduce.3.cloned.1.call-start = ((), (), s32[]{:S(2)}) async-start(), calls=%async_computation.1 | async-start | bytes 262144 | tf_op jit(solution)/shard_map/psum | solution.py:67
  367.6 62.9 %copy-start.3 = (bf16[4096,256]{1,0:T(8,128)(2,1)S(1)}, bf16[4096,256]{1,0:T(8,128)(2,1)}, u32[]{:S(2)}) copy-start(bf16[4096,256]{1,0:T(8,128)(2,1)} %all-gather.2.cloned.1.call-done) | copy-start | bytes 6291460
Sparse Core Ops, SparseCore 0:
  279.0 11.3 all-gather.1
  294.0 70.9 all-reduce.2
where the time goes:
time: 442 us; the launch traced here: 441 us
  other arithmetic  172 us (39%)
  waiting for transfers between devices  97 us (22%)
  local copies, waits for them, and re-layouts  86.9 us (20%)
  starting transfers between devices  46 us (10%)
  matrix products  18.4 us (4%)
  between operations  17.8 us (4%)
    scatter-add x2, other arithmetic, apply_operator(): jax.ops.segment_sum(products.reshape(-1, columns), flat_maps, num_segment...  91.9 us
    psum x1, waiting for transfers between devices, on_device(): margin_part = lax.psum(margin_part, 'dom')  71 us
    gather x2, local copies, waits for them, and re-layouts, apply_operator(): gathered = extended[cell_nodes]  59 us
    ppermute x16, starting transfers between devices, passed_along(): return lax.ppermute(value, axis, pairs)  46 us
    another operation x6, other arithmetic, on_device(): factor = jnp.linalg.cholesky(margin)  34 us
    another operation x3, other arithmetic, on_device(): lax.linalg.triangular_solve(factor, jnp.eye(band_count, dtype=factor.dtyp...  20.5 us
    scatter-add x2, other arithmetic, apply_operator(): jax.ops.segment_sum(jnp.stack(returned).reshape(-1, columns), targets, nu...  16.3 us
    ppermute x16, waiting for transfers between devices, passed_along(): return lax.ppermute(value, axis, pairs)  14.5 us
  transfers between devices with their start and end apart: 18, of which 9 were waited for; matrix products, arithmetic and copies ran while one was open for 0% of the time, Pallas kernels for 0%

commit v1 on v0

v1 whole, which is shorter than its diff:
```python
import functools

import jax
import jax.numpy as jnp
from jax import lax
from jax.experimental import pallas as pl
from jax.experimental.pallas import tpu as pltpu
from jax.sharding import PartitionSpec as P

peer_offsets = (1, -1, 2, -2)
MESH = pl.DeviceIdType.MESH
VM = pl.BlockSpec(memory_space=pltpu.VMEM)
SM = pl.BlockSpec(memory_space=pltpu.SMEM)
ACCS = 8


def params(**more):
    return pltpu.CompilerParams(vmem_limit_bytes=50 * 1024 * 1024, **more)


def chunks(total, size, body):
    def step(i, carry):
        body(pl.ds(pl.multiple_of(i * size, size), size))
        return carry

    lax.fori_loop(0, total // size, step, 0)


def exchange_kernel(sign, send_ref, recv_ref, send_sem, recv_sem):
    me = lax.axis_index("dom")
    size = lax.axis_size("dom")
    slot = send_ref.shape[0] // 4
    barrier = pltpu.get_barrier_semaphore()

    def exists(by):
        there = me + by
        return jnp.logical_and(there >= 0, there < size)

    for by in peer_offsets:

        @pl.when(exists(by))
        def _():
            pl.semaphore_signal(
                barrier, inc=1, device_id={"dom": me + by}, device_id_type=MESH
            )

    peers = jnp.int32(0)
    for by in peer_offsets:
        peers = peers + exists(by).astype(jnp.int32)
    pl.semaphore_wait(barrier, peers)

    def copy(o, by):
        rows = pl.ds(o * slot, slot)
        return pltpu.make_async_remote_copy(
            src_ref=send_ref.at[rows],
            dst_ref=recv_ref.at[rows],
            send_sem=send_sem.at[o],
            recv_sem=recv_sem.at[o],
            device_id={"dom": me + by},
            device_id_type=MESH,
        )

    for o in (2, 3, 0, 1):
        by = sign * peer_offsets[o]

        @pl.when(exists(by))
        def _():
            copy(o, by).start()

    for o in range(4):
        by = sign * peer_offsets[o]

        @pl.when(jnp.logical_not(exists(-by)))
        def _():
            recv_ref[pl.ds(o * slot, slot), :] = jnp.zeros(
                (slot, recv_ref.shape[1]), recv_ref.dtype
            )

    for o in range(4):
        by = sign * peer_offsets[o]

        @pl.when(exists(by))
        def _():
            copy(o, by).wait_send()

        @pl.when(exists(-by))
        def _():
            copy(o, by).wait_recv()


def exchange(values, sign):
    return pl.pallas_call(
        functools.partial(exchange_kernel, sign),
        out_shape=jax.ShapeDtypeStruct(values.shape, values.dtype),
        in_specs=[VM],
        out_specs=VM,
        scratch_shapes=[pltpu.SemaphoreType.DMA((4,)), pltpu.SemaphoreType.DMA((4,))],
        compiler_params=params(collective_id=1 if sign > 0 else 2, has_side_effects=True),
        name="exchange_out" if sign > 0 else "exchange_back",
    )(values)


def gather_faces(wide, targets_ref, stage, out_ref):
    group = 16

    def step(i, carry):
        base = pl.multiple_of(i * group, group)
        rows = [wide[pl.ds(targets_ref[base + u], 1), :] for u in range(group)]
        for u in range(group):
            stage[pl.ds(base + u, 1), :] = rows[u]
        return carry

    lax.fori_loop(0, stage.shape[0] // group, step, 0)

    def cast(rows):
        out_ref[rows, :] = stage[rows, :].astype(out_ref.dtype)

    chunks(stage.shape[0], 128, cast)


def faces_kernel(v_ref, targets_ref, out_ref, wide, stage):
    nodes = v_ref.shape[0]

    def widen(rows):
        wide[rows, :] = v_ref[rows, :].astype(jnp.float32)

    chunks(nodes, 256, widen)
    wide[pl.ds(nodes, 8), :] = jnp.zeros((8, wide.shape[1]), jnp.float32)
    gather_faces(wide, targets_ref, stage, out_ref)


def faces_of(v, targets):
    nodes, columns = v.shape
    count = targets.shape[0]
    return pl.pallas_call(
        faces_kernel,
        out_shape=jax.ShapeDtypeStruct((count, columns), v.dtype),
        in_specs=[VM, SM],
        out_specs=VM,
        scratch_shapes=[
            pltpu.VMEM((nodes + 8, columns), jnp.float32),
            pltpu.VMEM((count, columns), jnp.float32),
        ],
        compiler_params=params(),
        name="faces",
    )(v, targets)


def operate_kernel(
    v_ref, ghost_ref, matrix_ref, maps_ref, scale_ref, own_ref, back_ref, ext, *rest
):
    nodes, columns = v_ref.shape
    ghosts = ghost_ref.shape[0]
    nc = matrix_ref.shape[0]
    cells = scale_ref.shape[0]
    group = 8
    gat, prod, accs = rest[:2], rest[2:4], rest[4:]

    def widen(rows):
        ext[rows, :] = v_ref[rows, :].astype(jnp.float32)

    chunks(nodes, 256, widen)
    for part in range(ghosts // 256):
        ext[pl.ds(nodes + part * 256, 256), :] = ghost_ref[pl.ds(part * 256, 256), :].astype(
            jnp.float32
        )

    def clear(rows):
        for acc in accs:
            acc[rows, :] = jnp.zeros((64, columns), jnp.float32)

    chunks(nodes + ghosts, 64, clear)

    def gather_step(pair, base):
        rows = [
            (u, h, ext[pl.ds(maps_ref[(2 * pair + h) * nc + base + u], 1), :])
            for u in range(group)
            for h in range(2)
        ]
        for u, h, row in rows:
            gat[h][pl.ds(base + u, 1), :] = row

    def scatter_step(pair, base):
        for first in range(0, group, ACCS // 2):
            spots = []
            for u in range(ACCS // 2):
                for h in range(2):
                    at = pl.ds(maps_ref[(2 * pair + h) * nc + base + first + u], 1)
                    acc = accs[2 * u + h]
                    spots.append(
                        (acc, at, acc[at, :] + prod[h][pl.ds(base + first + u, 1), :])
                    )
            for acc, at, value in spots:
                acc[at, :] = value

    def rows_loop(body):
        def step(i, carry):
            body(pl.multiple_of(i * group, group))
            return carry

        lax.fori_loop(0, nc // group, step, 0)

    def multiply(pair):
        both = jnp.concatenate([gat[0][...], gat[1][...]], 1).astype(jnp.bfloat16)
        result = jnp.dot(matrix_ref[...], both, preferred_element_type=jnp.float32)
        for h in range(2):
            prod[h][...] = (
                result[:, h * columns : (h + 1) * columns] * scale_ref[2 * pair + h]
            )

    rows_loop(lambda base: gather_step(0, base))

    def pair_step(pair, carry):
        multiply(pair)

        def both(base):
            gather_step(pair + 1, base)
            scatter_step(pair, base)

        rows_loop(both)
        return carry

    last = cells // 2 - 1
    lax.fori_loop(0, last, pair_step, 0)
    multiply(last)
    rows_loop(lambda base: scatter_step(last, base))

    def total(rows):
        value = accs[0][rows, :]
        for acc in accs[1:]:
            value = value + acc[rows, :]
        return value

    def collect(rows):
        own_ref[rows, :] = total(rows)

    chunks(nodes, 64, collect)
    for part in range(ghosts // 64):
        back_ref[pl.ds(part * 64, 64), :] = total(pl.ds(nodes + part * 64, 64))


def operate(v, ghosts, matrix, maps, scale):
    nodes, columns = v.shape
    count = ghosts.shape[0]
    nc = matrix.shape[0]
    return pl.pallas_call(
        operate_kernel,
        out_shape=(
            jax.ShapeDtypeStruct((nodes, columns), jnp.float32),
            jax.ShapeDtypeStruct((count, columns), jnp.float32),
        ),
        in_specs=[VM, VM, VM, SM, SM],
        out_specs=(VM, VM),
        scratch_shapes=[
            pltpu.VMEM((nodes + count, columns), jnp.float32),
        ]
        + [pltpu.VMEM((nc, columns), jnp.float32)] * 4
        + [pltpu.VMEM((nodes + count, columns), jnp.float32)] * ACCS,
        compiler_params=params(),
        name="operate",
    )(v, ghosts, matrix, maps, scale)


def combine_kernel(first, own_ref, back_ref, v_ref, w_ref, diag_ref, targets_ref, coef_ref, *rest):
    nodes, columns = v_ref.shape
    count = back_ref.shape[0]
    slot = count // 4
    if first:
        out_ref, faces_ref, wide, stage = rest[:4]
    else:
        out_ref = rest[0]
    accs = rest[-4:]
    group = 4

    def fill(rows):
        accs[0][rows, :] = own_ref[rows, :]
        for acc in accs[1:]:
            acc[rows, :] = jnp.zeros((64, columns), jnp.float32)

    chunks(nodes, 64, fill)

    def step(i, carry):
        for u in range(group):
            spots = []
            for o in range(4):
                row = i * group + u + o * slot
                at = pl.ds(targets_ref[row], 1)
                spots.append((accs[o], at, accs[o][at, :] + back_ref[pl.ds(row, 1), :]))
            for acc, at, value in spots:
                acc[at, :] = value
        return carry

    lax.fori_loop(0, slot // group, step, 0)
    coef = coef_ref[0]

    def finish(rows):
        total = (accs[0][rows, :] + accs[1][rows, :]) + (accs[2][rows, :] + accs[3][rows, :])
        image = total * coef + diag_ref[rows, :] * v_ref[rows, :].astype(jnp.float32)
        if first:
            value = image.astype(jnp.bfloat16)
            wide[rows, :] = value.astype(jnp.float32)
        else:
            value = (2.0 * image - w_ref[rows, :].astype(jnp.float32)).astype(jnp.bfloat16)
        out_ref[rows, :] = value

    chunks(nodes, 64, finish)
    if first:
        wide[pl.ds(nodes, 8), :] = jnp.zeros((8, columns), jnp.float32)
        gather_faces(wide, targets_ref, stage, faces_ref)


def combine(first, own, back, v, w, diag, targets, coef):
    nodes, columns = v.shape
    count = back.shape[0]
    value = jax.ShapeDtypeStruct((nodes, columns), jnp.bfloat16)
    faces = jax.ShapeDtypeStruct((count, columns), jnp.bfloat16)
    extra = [
        pltpu.VMEM((nodes + 8, columns), jnp.float32),
        pltpu.VMEM((count, columns), jnp.float32),
    ]
    return pl.pallas_call(
        functools.partial(combine_kernel, first),
        out_shape=(value, faces) if first else value,
        in_specs=[VM, VM, VM, VM, VM, SM, SM],
        out_specs=(VM, VM) if first else VM,
        scratch_shapes=(extra if first else [])
        + [pltpu.VMEM((nodes + 8, columns), jnp.float32)] * 4,
        compiler_params=params(),
        name="combine_one" if first else "combine_two",
    )(own, back, v, w, diag, targets, coef)


def margin_kernel(scaling, x_ref, other_ref, margin_ref, part, slots, send_sem, recv_sem):
    columns = x_ref.shape[1]
    nodes = x_ref.shape[0]
    half_rows = columns // 2
    me = lax.axis_index("dom")
    mine = lax.axis_index("band")
    size = lax.axis_size("dom")
    bits = size.bit_length() - 1
    partners = [{"band": 1 - mine}]
    for k in range(bits):
        bit = 1 << k
        partners.append({"dom": me + bit - 2 * bit * (lax.div(me, bit) % 2)})

    barrier = pltpu.get_barrier_semaphore()
    for partner in partners:
        pl.semaphore_signal(barrier, inc=1, device_id=partner, device_id_type=MESH)
    pl.semaphore_wait(barrier, len(partners))

    def send(at, src, dst, partner):
        copy = pltpu.make_async_remote_copy(
            src_ref=src,
            dst_ref=dst,
            send_sem=send_sem.at[at],
            recv_sem=recv_sem.at[at],
            device_id=partner,
            device_id_type=MESH,
        )
        copy.start()
        return copy

    panel = send(0, x_ref, other_ref, partners[0])
    size_k = 512

    def product(right, lanes):
        def step(i, total):
            rows = pl.ds(pl.multiple_of(i * size_k, size_k), size_k)
            return total + lax.dot_general(
                x_ref[rows, :],
                right[rows, :],
                (((0,), (0,)), ((), ())),
                preferred_element_type=jnp.float32,
            )

        part[:, lanes] = lax.fori_loop(
            0, nodes // size_k, step, jnp.zeros((columns, columns), jnp.float32)
        )

    product(x_ref, pl.ds(0, columns))
    panel.wait()
    product(other_ref, pl.ds(columns, columns))

    low = me % 2
    keep = pl.ds(pl.multiple_of(low * half_rows, half_rows), half_rows)
    give = pl.ds(pl.multiple_of((1 - low) * half_rows, half_rows), half_rows)
    copy = send(1, part.at[give], slots.at[0], partners[1])
    copy.wait()
    part[keep, :] += slots[0]
    for k in range(1, bits):
        copy = send(1 + k, part.at[keep], slots.at[k], partners[1 + k])
        copy.wait()
        part[keep, :] += slots[k]
    copy = send(1 + bits, part.at[keep], slots.at[bits], partners[1])
    copy.wait()
    part[give, :] = slots[bits]
    part[...] = part[...] * scaling
    rows_mine = pl.ds(pl.multiple_of(mine * columns, columns), columns)
    rows_other = pl.ds(pl.multiple_of((1 - mine) * columns, columns), columns)
    copy = send(2 + bits, part, margin_ref.at[rows_mine], partners[0])
    margin_ref[rows_mine, :] = part[...]
    copy.wait()


def margin_of(x, scaling):
    nodes, columns = x.shape
    size = lax.axis_size("dom")
    bits = size.bit_length() - 1
    return pl.pallas_call(
        functools.partial(margin_kernel, scaling),
        out_shape=(
            jax.ShapeDtypeStruct((nodes, columns), x.dtype),
            jax.ShapeDtypeStruct((2 * columns, 2 * columns), jnp.float32),
        ),
        in_specs=[VM],
        out_specs=(VM, VM),
        scratch_shapes=[
            pltpu.VMEM((columns, 2 * columns), jnp.float32),
            pltpu.VMEM((bits + 1, columns // 2, 2 * columns), jnp.float32),
            pltpu.SemaphoreType.DMA((bits + 3,)),
            pltpu.SemaphoreType.DMA((bits + 3,)),
        ],
        compiler_params=params(collective_id=3, has_side_effects=True),
        name="margin",
    )(x)


def on_device(wavefunctions, bounds, cell_matrix, cell_scale, potential, cell_nodes, face_nodes):
    nodes, columns = wavefunctions.shape
    targets = jnp.where(face_nodes >= 0, face_nodes, nodes).reshape(-1)
    maps = cell_nodes.reshape(-1)
    center = (bounds[0] + bounds[1]) / 2.0
    coef = 1.0 / ((bounds[1] - bounds[0]) / 2.0)
    diag = jnp.broadcast_to(((potential - center) * coef)[:, None], (nodes, columns))
    coef = coef.reshape(1)

    def apply_sums(vectors, faces):
        ghosts = exchange(faces, 1)
        own, back = operate(vectors, ghosts, cell_matrix, maps, cell_scale)
        return own, exchange(back, -1)

    own, back = apply_sums(wavefunctions, faces_of(wavefunctions, targets))
    one, faces = combine(True, own, back, wavefunctions, wavefunctions, diag, targets, coef)
    own, back = apply_sums(one, faces)
    two = combine(False, own, back, one, wavefunctions, diag, targets, coef)
    other, margin = margin_of(two, 1.0 / (nodes * lax.axis_size("dom")))
    mine = lax.axis_index("band")
    left, right = margin[:columns], margin[columns:]
    right = jnp.concatenate([right[:, columns:], right[:, :columns]], 1)
    margin = jnp.concatenate([left, right], 0)
    factor = jnp.linalg.cholesky(margin)
    band_count = margin.shape[0]
    inverse = lax.linalg.triangular_solve(
        factor, jnp.eye(band_count, dtype=factor.dtype), left_side=True, lower=True
    )
    own_rows = lax.dynamic_slice_in_dim(inverse, mine * columns, columns, 0)
    own_part = lax.dynamic_slice_in_dim(own_rows, mine * columns, columns, 1)
    other_part = lax.dynamic_slice_in_dim(own_rows, (1 - mine) * columns, columns, 1)
    panel = jnp.concatenate([two, other], 1)
    rows = jnp.concatenate([own_part, other_part], 1)
    high = rows.astype(jnp.bfloat16)
    low = (rows - high.astype(jnp.float32)).astype(jnp.bfloat16)
    return jnp.dot(panel, high.T, preferred_element_type=jnp.float32) + jnp.dot(
        panel, low.T, preferred_element_type=jnp.float32
    )


def solution(mesh):
    return jax.shard_map(
        on_device,
        mesh=mesh,
        in_specs=(
            P(("kpt", "dom"), "band"),
            P("kpt"),
            P(),
            P("dom"),
            P("dom"),
            P("dom", None),
            P("dom", None),
        ),
        out_specs=P(("kpt", "dom"), "band"),
        check_vma=False,
    )
```

time: 442 us -> 188 us (0.43)
  other arithmetic: 172 us -> 55 us
  Pallas kernels: 0 us -> 116 us
  waiting for transfers between devices: 97 us -> 0 us
  local copies, waits for them, and re-layouts: 86.9 us -> 7.85 us
  starting transfers between devices: 46 us -> 0 us
  matrix products: 18.4 us -> 4.04 us
  between operations: 17.8 us -> 4.34 us
    pallas_call x0 -> x10, Pallas kernels: none -> 116 us  [the longest x2 50.6 us: operate(): pl.pallas_call(operate_kernel, out_shape=(jax.ShapeDtypeStruct((nodes, co...]
    scatter-add x4 -> x0, other arithmetic: 108 us -> none  [the longest x2 91.9 us: apply_operator(): jax.ops.segment_sum(products.reshape(-1, columns), flat_maps, num_segment...]
    psum x1 -> x0, waiting for transfers between devices: 71 us -> none  [on_device(): margin_part = lax.psum(margin_part, 'dom')]
    gather x4 -> x0, local copies, waits for them, and re-layouts: 67.4 us -> none  [the longest x2 59 us: apply_operator(): gathered = extended[cell_nodes]]
    ppermute x16 -> x0, starting transfers between devices: 46 us -> none  [passed_along(): return lax.ppermute(value, axis, pairs)]
    ppermute x16 -> x0, waiting for transfers between devices: 14.5 us -> none  [passed_along(): return lax.ppermute(value, axis, pairs)]
    dot_general x4 -> x2, matrix products: 17.1 us -> 2.73 us  [the longest x1 2.04 us: on_device(): jnp.dot(panel, low.T, preferred_element_type=jnp.float32)]
    all_gather x1 -> x0, waiting for transfers between devices: 11.5 us -> none  [on_device(): panel_all = lax.all_gather(degree_two, 'band', axis=1, tiled=True)]
  transfers between devices with their start and end apart: 18 -> 0, of which waited for: 9 -> 0; matrix products, arithmetic and copies ran while one was open for 0% -> 0% of each run, Pallas kernels for 0% -> 0%
where the time goes in v1:
time: 188 us; the launch traced here: 187 us
  Pallas kernels  116 us (62%)
  other arithmetic  55 us (29%)
  local copies, waits for them, and re-layouts  7.85 us (4%)
  between operations  4.34 us (2%)
  matrix products  4.04 us (2%)
    pallas_call x2, Pallas kernels, operate(): pl.pallas_call(operate_kernel, out_shape=(jax.ShapeDtypeStruct((nodes, co...  50.6 us
    another operation x6, other arithmetic, on_device(): factor = jnp.linalg.cholesky(margin)  34 us
    pallas_call x4, Pallas kernels, exchange(): pl.pallas_call(functools.partial(exchange_kernel, sign), out_shape=jax.Sh...  28.1 us
    pallas_call x1, Pallas kernels, margin_of(): pl.pallas_call(functools.partial(margin_kernel, scaling), out_shape=(jax....  22.6 us
    another operation x4, other arithmetic, on_device(): lax.linalg.triangular_solve(factor, jnp.eye(band_count, dtype=factor.dtyp...  20.1 us
    pallas_call x2, Pallas kernels, combine(): pl.pallas_call(functools.partial(combine_kernel, first), out_shape=(value...  13 us
    another operation x6, local copies, waits for them, and re-layouts  4.02 us

profile of v1, /device:TPU:0, one launch (start us, length us, event | category | flops | bytes accessed | tf_op | source)
XLA Modules:
  0.0 187.4 jit_solution(3916923168025708042)
XLA Ops:
  0.0 0.0 copy-start.4
  0.0 0.0 copy-start
  0.0 0.0 copy-start.3
  0.0 0.0 copy-start.2
  0.0 0.0 copy-start.1
  0.0 1.5 fusion.20
  4.2 0.7 subtract_multiply_fusion
  4.9 2.0 %broadcast_in_dim.13.diag_ref = f32[4096,128]{1,0:T(8,128)} broadcast(f32[4096]{0:T(1024)S(1)} %subtract_multiply_fusion), dimensions={0} | broadcast | bytes 2113536 | tf_op jit(solution)/shard_map/broadcast_in_dim | solution.py:434
  6.9 0.0 copy-done.4
  6.9 0.0 copy-done
  6.9 2.0 %faces.1.send_ref = bf16[1024,128]{1,0:T(8,128)(2,1)S(1)} custom-call(bf16[4096,128]{1,0:T(8,128)(2,1)S(1)} %copy-done, s32[1024]{0:T(1024)S(1)} %bitcast.40), custom_call_target="tpu_custom_call" | custom-call | tf_op jit(solution)/shard_map/faces/pallas_call | solution.py:135
  8.9 7.3 %exchange_out.2.ghost_ref = bf16[1024,128]{1,0:T(8,128)(2,1)S(1)} custom-call(bf16[1024,128]{1,0:T(8,128)(2,1)S(1)} %faces.1.send_ref), custom_call_target="tpu_custom_call" | custom-call | tf_op jit(solution)/shard_map/exchange_out/pallas_call | solution.py:92
  16.2 0.0 copy-done.3
  16.2 0.0 copy-done.2
  16.2 0.0 copy-done.1
  16.2 25.3 %operate.2 = (f32[4096,128]{1,0:T(8,128)}, f32[1024,128]{1,0:T(8,128)S(1)}) custom-call(bf16[4096,128]{1,0:T(8,128)(2,1)S(1)} %copy-done, bf16[1024,128]{1,0:T(8,128)(2,1)S(1)} %exchange_out.2.ghost_ref, bf16[512,512]{1,0:T(8,128)(2,1)S(1)} %copy-done.1, s32[8192]{0:T(1024)S(1)} %bitcast.38, f32[16]{0:T(128)S(1)} %copy-done.2), custom_call_target="tpu_custom_call" | custom-call | tf_op jit(solution)/shard_map/operate/pallas_call | solution.py:246
  41.5 7.3 %exchange_back.2.back_ref = f32[1024,128]{1,0:T(8,128)S(1)} custom-call(f32[1024,128]{1,0:T(8,128)S(1)} %get-tuple-element.14.send_ref), custom_call_target="tpu_custom_call" | custom-call | tf_op jit(solution)/shard_map/exchange_back/pallas_call | solution.py:92
  48.8 7.0 %combine_one.1 = (bf16[4096,128]{1,0:T(8,128)(2,1)S(1)}, bf16[1024,128]{1,0:T(8,128)(2,1)S(1)}) custom-call(f32[4096,128]{1,0:T(8,128)} %get-tuple-element.13.own_ref, f32[1024,128]{1,0:T(8,128)S(1)} %exchange_back.2.back_ref, bf16[4096,128]{1,0:T(8,128)(2,1)S(1)} %copy-done, bf16[4096,128]{1,0:T(8,128)(2,1)S(1)} %copy-done, ...), custom_call_target="tpu_custom_call" | custom-call | tf_op jit(solution)/shard_map/combine_one/pallas_call | solution.py:321
  55.8 6.8 %exchange_out.3.ghost_ref = bf16[1024,128]{1,0:T(8,128)(2,1)S(1)} custom-call(bf16[1024,128]{1,0:T(8,128)(2,1)S(1)} %get-tuple-element.16.send_ref), custom_call_target="tpu_custom_call" | custom-call | tf_op jit(solution)/shard_map/exchange_out/pallas_call | solution.py:92
  62.7 25.3 %operate.3 = (f32[4096,128]{1,0:T(8,128)}, f32[1024,128]{1,0:T(8,128)S(1)}) custom-call(bf16[4096,128]{1,0:T(8,128)(2,1)S(1)} %get-tuple-element.15.v_ref, bf16[1024,128]{1,0:T(8,128)(2,1)S(1)} %exchange_out.3.ghost_ref, bf16[512,512]{1,0:T(8,128)(2,1)S(1)} %copy-done.1, s32[8192]{0:T(1024)S(1)} %bitcast.39, f32[16]{0:T(128)S(1)} %copy-done.2), custom_call_target="tpu_custom_call" | custom-call | tf_op jit(solution)/shard_map/operate/pallas_call | solution.py:246
  88.0 6.7 %exchange_back.3.back_ref = f32[1024,128]{1,0:T(8,128)S(1)} custom-call(f32[1024,128]{1,0:T(8,128)S(1)} %get-tuple-element.18.send_ref), custom_call_target="tpu_custom_call" | custom-call | tf_op jit(solution)/shard_map/exchange_back/pallas_call | solution.py:92
  94.7 6.0 %combine_two.1.x_ref = bf16[4096,128]{1,0:T(8,128)(2,1)S(1)} custom-call(f32[4096,128]{1,0:T(8,128)} %get-tuple-element.17.own_ref, f32[1024,128]{1,0:T(8,128)S(1)} %exchange_back.3.back_ref, bf16[4096,128]{1,0:T(8,128)(2,1)S(1)} %get-tuple-element.15.v_ref, bf16[4096,128]{1,0:T(8,128)(2,1)S(1)} %copy-done, f32[4096,128]{1,0:T(8,128)} %broadcast_in_dim.13.diag_ref, ...), custom_call_target="tpu_custom_call" | custom-call | tf_op jit(solution)/shard_map/combine_two/pallas_call | solution.py:321
  100.6 22.6 %margin.1 = (bf16[4096,128]{1,0:T(8,128)(2,1)S(1)}, f32[256,256]{1,0:T(8,128)S(1)}) custom-call(bf16[4096,128]{1,0:T(8,128)(2,1)S(1)} %combine_two.1.x_ref), custom_call_target="tpu_custom_call" | custom-call | tf_op jit(solution)/shard_map/margin/pallas_call | solution.py:409
  123.2 0.1 copy.8
  123.4 0.1 copy.11
  123.6 11.7 %cholesky.50 = f32[128,128]{1,0:T(8,128)S(1)} custom-call(f32[128,128]{1,0:T(8,128)S(1)} %cholesky.118), custom_call_target="Cholesky" | custom-call | tf_op jit(solution)/shard_map/jit(cholesky)/cholesky | solution.py:451
  135.4 9.8 %custom-call.14 = f32[1,128,128]{1,2,0:T(8,128)S(1)} custom-call(f32[1,128,128]{2,1,0:T(8,128)S(1)} %get-tuple-element.46), custom_call_target="InvertDiagBlocksLowerTriangular" | custom-call | tf_op jit(solution)/shard_map/jit(cholesky)/cholesky | solution.py:451
  145.2 0.2 constant_dynamic-update-slice_fusion.1
  145.4 0.3 convolution_subtract_fusion.1
  145.7 11.7 %cholesky.105 = f32[128,128]{1,0:T(8,128)S(1)} custom-call(f32[128,128]{1,0:T(8,128)S(1)} %convolution_subtract_fusion.1), custom_call_target="Cholesky" | custom-call | tf_op jit(solution)/shard_map/jit(cholesky)/cholesky | solution.py:451
  157.4 0.7 compare_reduce_fusion
  159.6 0.1 triangular_solve.63
  159.6 4.1 %while.1 = (s32[]{:T(128)}, f32[256,256]{1,0:T(8,128)S(1)}, s32[2,2]{1,0:T(2,128)S(1)}, f32[2,128,128]{2,1,0:T(8,128)S(1)}, s32[]{:T(128)}) while((s32[]{:T(128)}, f32[256,256]{1,0:T(8,128)S(1)}, s32[2,2]{1,0:T(2,128)S(1)}, f32[2,128,128]{2,1,0:T(8,128)S(1)}, s32[]{:T(128)}) %tuple.26), condition=%wide.while_cond, body=%wide.while_body.sunk | while | flops 2 | bytes 131181 | solution.py:453
  159.6 0.7 fusion.26
  160.3 1.3 bitcast_dynamic-update-slice_fusion.2
  161.7 0.7 fusion.26
  162.3 1.3 bitcast_dynamic-update-slice_fusion.2
  163.7 19.9 %custom-call.15 = f32[2,128,128]{1,2,0:T(8,128)S(1)} custom-call(f32[2,128,128]{2,1,0:T(8,128)S(1)} %get-tuple-element.28), custom_call_target="InvertDiagBlocksLowerTriangular" | custom-call | tf_op jit(solution)/shard_map/triangular_solve | solution.py:453
  183.6 0.3 fusion.2
  183.9 0.3 convolution_subtract_fusion
  184.2 0.3 fusion.9
  184.5 0.2 fusion.7
  184.7 0.7 fusion
  185.4 2.0 %convolution_add_fusion = f32[4096,128]{1,0:T(8,128)} fusion(f32[4096,128]{1,0:T(8,128)S(1)} %fusion, bf16[4096,128]{1,0:T(8,128)(2,1)S(1)} %get-tuple-element.19, bf16[4096,128]{1,0:T(8,128)(2,1)S(1)} %combine_two.1.x_ref, f32[128,128]{1,0:T(8,128)S(1)} %get-tuple-element.40, f32[128,128]{1,0:T(8,128)S(1)} %get-tuple-element.39), kind=kOutput, calls=%fused_computation.2 | convolution fusion | flops 273317888 | bytes 6422528 | tf_op jit(solution)/shard_map/dot_general | solution.py:463
  (17 shorter events, 0.3 us)
Async XLA Ops:
  0.0 6.9 %copy-start.4 = (s32[4,256]{1,0:T(4,128)S(1)}, s32[4,256]{1,0:T(4,128)}, u32[]{:S(2)}) copy-start(s32[4,256]{1,0:T(4,128)} %param.13) | copy-start | bytes 12292
  0.0 6.9 %copy-start = (bf16[4096,128]{1,0:T(8,128)(2,1)S(1)}, bf16[4096,128]{1,0:T(8,128)(2,1)}, u32[]{:S(2)}) copy-start(bf16[4096,128]{1,0:T(8,128)(2,1)} %w_ref.3) | copy-start | bytes 3145732
  0.0 16.2 %copy-start.3 = (s32[16,512]{1,0:T(8,128)S(1)}, s32[16,512]{1,0:T(8,128)}, u32[]{:S(2)}) copy-start(s32[16,512]{1,0:T(8,128)} %param.12) | copy-start | bytes 98308
  0.0 16.2 %copy-start.2 = (f32[16]{0:T(128)S(1)}, f32[16]{0:T(128)}, u32[]{:S(2)}) copy-start(f32[16]{0:T(128)} %scale_ref.3) | copy-start | bytes 196
  0.0 16.2 %copy-start.1 = (bf16[512,512]{1,0:T(8,128)(2,1)S(1)}, bf16[512,512]{1,0:T(8,128)(2,1)}, u32[]{:S(2)}) copy-start(bf16[512,512]{1,0:T(8,128)(2,1)} %matrix_ref.3) | copy-start | bytes 1572868

commit v2 on v1

--- a/solution.py
+++ b/solution.py
@@ -394,11 +394,11 @@
     copy = send(1 + bits, part.at[keep], slots.at[bits], partners[1])
     copy.wait()
     part[give, :] = slots[bits]
-    part[...] = part[...] * scaling
     rows_mine = pl.ds(pl.multiple_of(mine * columns, columns), columns)
-    rows_other = pl.ds(pl.multiple_of((1 - mine) * columns, columns), columns)
-    copy = send(2 + bits, part, margin_ref.at[rows_mine], partners[0])
-    margin_ref[rows_mine, :] = part[...]
+    lanes_other = pl.ds(pl.multiple_of((1 - mine) * columns, columns), columns)
+    margin_ref[rows_mine, rows_mine] = part[:, :columns] * scaling
+    margin_ref[rows_mine, lanes_other] = part[:, columns:] * scaling
+    copy = send(2 + bits, margin_ref.at[rows_mine], margin_ref.at[rows_mine], partners[0])
     copy.wait()
 
 
@@ -425,6 +425,89 @@
     )(x)
 
 
+BLOCK = 64
+
+
+def inverse_factor(block):
+    lane = lax.broadcasted_iota(jnp.int32, (8, 2 * BLOCK), 1)
+    sub = lax.broadcasted_iota(jnp.int32, (8, 2 * BLOCK), 0)
+    doubled = jnp.concatenate([block, block], 1)
+    tiles = []
+    for t in range(BLOCK // 8):
+        unit = (lane - BLOCK == sub + 8 * t).astype(jnp.float32)
+        tiles.append(jnp.where(lane < BLOCK, doubled[8 * t : 8 * t + 8], unit))
+    for j in range(BLOCK):
+        t, u = divmod(j, 8)
+        columns = {i: jnp.broadcast_to(tiles[i][:, j : j + 1], (8, 2 * BLOCK)) for i in range(t, BLOCK // 8)}
+        pivot = jnp.broadcast_to(columns[t][u : u + 1], (8, 2 * BLOCK))
+        row = jnp.broadcast_to(tiles[t][u : u + 1], (8, 2 * BLOCK)) / pivot
+        tiles[t] = tiles[t] - jnp.where(sub > u, columns[t], 0.0) * row
+        for i in range(t + 1, BLOCK // 8):
+            tiles[i] = tiles[i] - columns[i] * row
+    scaled = []
+    for t, tile in enumerate(tiles):
+        diagonal = jnp.sum(jnp.where(lane == sub + 8 * t, tile, 0.0), 1, keepdims=True)
+        scaled.append(tile * lax.rsqrt(diagonal))
+    return jnp.concatenate(scaled, 0)[:, BLOCK:]
+
+
+def finish_kernel(margin_ref, x_ref, other_ref, mine_ref, out_ref, work):
+    nodes, columns = x_ref.shape
+    bands = margin_ref.shape[0]
+    exact = lax.Precision.HIGHEST
+    work[...] = margin_ref[...]
+    for first in range(0, bands, BLOCK):
+        last = first + BLOCK
+        inverse = inverse_factor(work[first:last, first:last])
+        pieces = [inverse]
+        if first:
+            pieces = [work[first:last, :first]] + pieces
+        if last < bands:
+            pieces = pieces + [work[first:last, last:]]
+        for at, piece in enumerate(pieces):
+            if piece is not inverse:
+                pieces[at] = jnp.dot(inverse, piece, precision=exact)
+        row = jnp.concatenate(pieces, 1) if len(pieces) > 1 else pieces[0]
+        lane = lax.broadcasted_iota(jnp.int32, (BLOCK, bands), 1)
+        work[first:last, :] = jnp.where(lane < last, row, 0.0)
+        if last < bands:
+            update = lax.dot_general(
+                row[:, last:], row, (((0,), (0,)), ((), ())), precision=exact
+            )
+            lane = lax.broadcasted_iota(jnp.int32, (bands - last, bands), 1)
+            fresh = jnp.logical_and(lane >= first, lane < last)
+            work[last:, :] = jnp.where(fresh, 0.0, work[last:, :]) - update
+
+    mine = mine_ref[0]
+    own_at = pl.ds(pl.multiple_of(mine * columns, columns), columns)
+    other_at = pl.ds(pl.multiple_of((1 - mine) * columns, columns), columns)
+    rows = jnp.concatenate([work[own_at, own_at], work[own_at, other_at]], 1)
+    high = rows.astype(jnp.bfloat16)
+    low = (rows - high.astype(jnp.float32)).astype(jnp.bfloat16)
+    both = jnp.concatenate([high, low], 0)
+
+    def rotate(at):
+        panel = jnp.concatenate([x_ref[at, :], other_ref[at, :]], 1)
+        value = lax.dot_general(
+            panel, both, (((1,), (1,)), ((), ())), preferred_element_type=jnp.float32
+        )
+        out_ref[at, :] = value[:, :columns] + value[:, columns:]
+
+    chunks(nodes, 512, rotate)
+
+
+def finish(margin, x, other, mine):
+    return pl.pallas_call(
+        finish_kernel,
+        out_shape=jax.ShapeDtypeStruct(x.shape, jnp.float32),
+        in_specs=[VM, VM, VM, SM],
+        out_specs=VM,
+        scratch_shapes=[pltpu.VMEM(margin.shape, jnp.float32)],
+        compiler_params=params(),
+        name="finish",
+    )(margin, x, other, mine)
+
+
 def on_device(wavefunctions, bounds, cell_matrix, cell_scale, potential, cell_nodes, face_nodes):
     nodes, columns = wavefunctions.shape
     targets = jnp.where(face_nodes >= 0, face_nodes, nodes).reshape(-1)
@@ -444,25 +527,7 @@
     own, back = apply_sums(one, faces)
     two = combine(False, own, back, one, wavefunctions, diag, targets, coef)
     other, margin = margin_of(two, 1.0 / (nodes * lax.axis_size("dom")))
-    mine = lax.axis_index("band")
-    left, right = margin[:columns], margin[columns:]
-    right = jnp.concatenate([right[:, columns:], right[:, :columns]], 1)
-    margin = jnp.concatenate([left, right], 0)
-    factor = jnp.linalg.cholesky(margin)
-    band_count = margin.shape[0]
-    inverse = lax.linalg.triangular_solve(
-        factor, jnp.eye(band_count, dtype=factor.dtype), left_side=True, lower=True
-    )
-    own_rows = lax.dynamic_slice_in_dim(inverse, mine * columns, columns, 0)
-    own_part = lax.dynamic_slice_in_dim(own_rows, mine * columns, columns, 1)
-    other_part = lax.dynamic_slice_in_dim(own_rows, (1 - mine) * columns, columns, 1)
-    panel = jnp.concatenate([two, other], 1)
-    rows = jnp.concatenate([own_part, other_part], 1)
-    high = rows.astype(jnp.bfloat16)
-    low = (rows - high.astype(jnp.float32)).astype(jnp.bfloat16)
-    return jnp.dot(panel, high.T, preferred_element_type=jnp.float32) + jnp.dot(
-        panel, low.T, preferred_element_type=jnp.float32
-    )
+    return finish(margin, two, other, lax.axis_index("band").reshape(1))
 
 
 def solution(mesh):

time: 188 us -> 163 us (0.87)
  other arithmetic: 55 us -> 0.73 us
  Pallas kernels: 116 us -> 156 us
  local copies, waits for them, and re-layouts: 7.85 us -> 3.41 us
  matrix products: 4.04 us -> 0 us
    another operation x10 -> x0, other arithmetic: 54.2 us -> none  [the longest x6 34 us: on_device(): factor = jnp.linalg.cholesky(margin)]
    pallas_call x0 -> x1, Pallas kernels: none -> 39.9 us  [finish(): pl.pallas_call(finish_kernel, out_shape=jax.ShapeDtypeStruct(x.shape, jnp...]
    another operation x9 -> x0, local copies, waits for them, and re-layouts: 4.12 us -> none
    dot_general x2 -> x0, matrix products: 2.73 us -> none  [the longest x1 2.04 us: on_device(): jnp.dot(panel, low.T, preferred_element_type=jnp.float32)]
where the time goes in v2:
time: 163 us
  Pallas kernels  156 us (96%)
  local copies, waits for them, and re-layouts  3.41 us (2%)
  between operations  2.7 us (2%)
    pallas_call x2, Pallas kernels, operate(): pl.pallas_call(operate_kernel, out_shape=(jax.ShapeDtypeStruct((nodes, co...  50.6 us
    pallas_call x1, Pallas kernels, finish(): pl.pallas_call(finish_kernel, out_shape=jax.ShapeDtypeStruct(x.shape, jnp...  39.9 us
    pallas_call x4, Pallas kernels, exchange(): pl.pallas_call(functools.partial(exchange_kernel, sign), out_shape=jax.Sh...  28 us
    pallas_call x1, Pallas kernels, margin_of(): pl.pallas_call(functools.partial(margin_kernel, scaling), out_shape=(jax....  22.5 us
    pallas_call x2, Pallas kernels, combine(): pl.pallas_call(functools.partial(combine_kernel, first), out_shape=(value...  13.1 us

profile of v2, /device:TPU:0, one launch (start us, length us, event | category | flops | bytes accessed | tf_op | source)
XLA Modules:
  0.0 162.9 jit_solution(7428163759572111707)
XLA Ops:
  0.0 0.0 copy-start.4
  0.0 0.0 copy-start
  0.0 0.0 copy-start.3
  0.0 0.0 copy-start.2
  0.0 0.0 copy-start.1
  0.0 1.4 fusion.1
  4.0 0.7 subtract_multiply_fusion
  4.8 1.9 %broadcast_in_dim.11.diag_ref = f32[4096,128]{1,0:T(8,128)} broadcast(f32[4096]{0:T(1024)S(1)} %subtract_multiply_fusion), dimensions={0} | broadcast | bytes 2113536 | tf_op jit(solution)/shard_map/broadcast_in_dim | solution.py:517
  6.7 0.0 copy-done.4
  6.7 0.0 copy-done
  6.7 2.0 %faces.1.send_ref = bf16[1024,128]{1,0:T(8,128)(2,1)S(1)} custom-call(bf16[4096,128]{1,0:T(8,128)(2,1)S(1)} %copy-done, s32[1024]{0:T(1024)S(1)} %bitcast.10), custom_call_target="tpu_custom_call" | custom-call | tf_op jit(solution)/shard_map/faces/pallas_call | solution.py:135
  8.7 7.3 %exchange_out.2.ghost_ref = bf16[1024,128]{1,0:T(8,128)(2,1)S(1)} custom-call(bf16[1024,128]{1,0:T(8,128)(2,1)S(1)} %faces.1.send_ref), custom_call_target="tpu_custom_call" | custom-call | tf_op jit(solution)/shard_map/exchange_out/pallas_call | solution.py:92
  16.0 0.0 copy-done.3
  16.0 0.0 copy-done.2
  16.0 0.0 copy-done.1
  16.0 25.3 %operate.2 = (f32[4096,128]{1,0:T(8,128)}, f32[1024,128]{1,0:T(8,128)S(1)}) custom-call(bf16[4096,128]{1,0:T(8,128)(2,1)S(1)} %copy-done, bf16[1024,128]{1,0:T(8,128)(2,1)S(1)} %exchange_out.2.ghost_ref, bf16[512,512]{1,0:T(8,128)(2,1)S(1)} %copy-done.1, s32[8192]{0:T(1024)S(1)} %bitcast.8, f32[16]{0:T(128)S(1)} %copy-done.2), custom_call_target="tpu_custom_call" | custom-call | tf_op jit(solution)/shard_map/operate/pallas_call | solution.py:246
  41.3 7.3 %exchange_back.2.back_ref = f32[1024,128]{1,0:T(8,128)S(1)} custom-call(f32[1024,128]{1,0:T(8,128)S(1)} %get-tuple-element.14.send_ref), custom_call_target="tpu_custom_call" | custom-call | tf_op jit(solution)/shard_map/exchange_back/pallas_call | solution.py:92
  48.6 7.1 %combine_one.1 = (bf16[4096,128]{1,0:T(8,128)(2,1)S(1)}, bf16[1024,128]{1,0:T(8,128)(2,1)S(1)}) custom-call(f32[4096,128]{1,0:T(8,128)} %get-tuple-element.13.own_ref, f32[1024,128]{1,0:T(8,128)S(1)} %exchange_back.2.back_ref, bf16[4096,128]{1,0:T(8,128)(2,1)S(1)} %copy-done, bf16[4096,128]{1,0:T(8,128)(2,1)S(1)} %copy-done, ...), custom_call_target="tpu_custom_call" | custom-call | tf_op jit(solution)/shard_map/combine_one/pallas_call | solution.py:321
  55.7 6.7 %exchange_out.3.ghost_ref = bf16[1024,128]{1,0:T(8,128)(2,1)S(1)} custom-call(bf16[1024,128]{1,0:T(8,128)(2,1)S(1)} %get-tuple-element.16.send_ref), custom_call_target="tpu_custom_call" | custom-call | tf_op jit(solution)/shard_map/exchange_out/pallas_call | solution.py:92
  62.4 25.3 %operate.3 = (f32[4096,128]{1,0:T(8,128)}, f32[1024,128]{1,0:T(8,128)S(1)}) custom-call(bf16[4096,128]{1,0:T(8,128)(2,1)S(1)} %get-tuple-element.15.v_ref, bf16[1024,128]{1,0:T(8,128)(2,1)S(1)} %exchange_out.3.ghost_ref, bf16[512,512]{1,0:T(8,128)(2,1)S(1)} %copy-done.1, s32[8192]{0:T(1024)S(1)} %bitcast.9, f32[16]{0:T(128)S(1)} %copy-done.2), custom_call_target="tpu_custom_call" | custom-call | tf_op jit(solution)/shard_map/operate/pallas_call | solution.py:246
  87.7 6.7 %exchange_back.3.back_ref = f32[1024,128]{1,0:T(8,128)S(1)} custom-call(f32[1024,128]{1,0:T(8,128)S(1)} %get-tuple-element.18.send_ref), custom_call_target="tpu_custom_call" | custom-call | tf_op jit(solution)/shard_map/exchange_back/pallas_call | solution.py:92
  94.4 6.0 %combine_two.1.x_ref = bf16[4096,128]{1,0:T(8,128)(2,1)S(1)} custom-call(f32[4096,128]{1,0:T(8,128)} %get-tuple-element.17.own_ref, f32[1024,128]{1,0:T(8,128)S(1)} %exchange_back.3.back_ref, bf16[4096,128]{1,0:T(8,128)(2,1)S(1)} %get-tuple-element.15.v_ref, bf16[4096,128]{1,0:T(8,128)(2,1)S(1)} %copy-done, f32[4096,128]{1,0:T(8,128)} %broadcast_in_dim.11.diag_ref, ...), custom_call_target="tpu_custom_call" | custom-call | tf_op jit(solution)/shard_map/combine_two/pallas_call | solution.py:321
  100.5 22.5 %margin.1 = (bf16[4096,128]{1,0:T(8,128)(2,1)S(1)}, f32[256,256]{1,0:T(8,128)S(1)}) custom-call(bf16[4096,128]{1,0:T(8,128)(2,1)S(1)} %combine_two.1.x_ref), custom_call_target="tpu_custom_call" | custom-call | tf_op jit(solution)/shard_map/margin/pallas_call | solution.py:409
  123.0 39.9 %finish.1 = f32[4096,128]{1,0:T(8,128)} custom-call(f32[256,256]{1,0:T(8,128)S(1)} %get-tuple-element.19.margin_ref, bf16[4096,128]{1,0:T(8,128)(2,1)S(1)} %combine_two.1.x_ref, bf16[4096,128]{1,0:T(8,128)(2,1)S(1)} %get-tuple-element.20.other_ref, s32[1]{0:T(128)} %bitcast.2.mine_ref), custom_call_target="tpu_custom_call" | custom-call | tf_op jit(solution)/shard_map/finish/pallas_call | solution.py:500
  (3 shorter events, 0.0 us)
Async XLA Ops:
  0.0 6.7 %copy-start.4 = (s32[4,256]{1,0:T(4,128)S(1)}, s32[4,256]{1,0:T(4,128)}, u32[]{:S(2)}) copy-start(s32[4,256]{1,0:T(4,128)} %param.13) | copy-start | bytes 12292
  0.0 6.7 %copy-start = (bf16[4096,128]{1,0:T(8,128)(2,1)S(1)}, bf16[4096,128]{1,0:T(8,128)(2,1)}, u32[]{:S(2)}) copy-start(bf16[4096,128]{1,0:T(8,128)(2,1)} %w_ref.3) | copy-start | bytes 3145732
  0.0 16.0 %copy-start.3 = (s32[16,512]{1,0:T(8,128)S(1)}, s32[16,512]{1,0:T(8,128)}, u32[]{:S(2)}) copy-start(s32[16,512]{1,0:T(8,128)} %param.12) | copy-start | bytes 98308
  0.0 16.0 %copy-start.2 = (f32[16]{0:T(128)S(1)}, f32[16]{0:T(128)}, u32[]{:S(2)}) copy-start(f32[16]{0:T(128)} %scale_ref.3) | copy-start | bytes 196
  0.0 16.0 %copy-start.1 = (bf16[512,512]{1,0:T(8,128)(2,1)S(1)}, bf16[512,512]{1,0:T(8,128)(2,1)}, u32[]{:S(2)}) copy-start(bf16[512,512]{1,0:T(8,128)(2,1)} %matrix_ref.3) | copy-start | bytes 1572868

commit v3 on v2

--- a/solution.py
+++ b/solution.py
@@ -26,16 +26,13 @@
     lax.fori_loop(0, total // size, step, 0)
 
 
-def exchange_kernel(sign, send_ref, recv_ref, send_sem, recv_sem):
+def exists(by):
+    there = lax.axis_index("dom") + by
+    return jnp.logical_and(there >= 0, there < lax.axis_size("dom"))
+
+
+def greet_neighbours(barrier):
     me = lax.axis_index("dom")
-    size = lax.axis_size("dom")
-    slot = send_ref.shape[0] // 4
-    barrier = pltpu.get_barrier_semaphore()
-
-    def exists(by):
-        there = me + by
-        return jnp.logical_and(there >= 0, there < size)
-
     for by in peer_offsets:
 
         @pl.when(exists(by))
@@ -44,105 +41,125 @@
                 barrier, inc=1, device_id={"dom": me + by}, device_id_type=MESH
             )
 
+
+def await_neighbours(barrier):
     peers = jnp.int32(0)
     for by in peer_offsets:
         peers = peers + exists(by).astype(jnp.int32)
     pl.semaphore_wait(barrier, peers)
 
-    def copy(o, by):
-        rows = pl.ds(o * slot, slot)
-        return pltpu.make_async_remote_copy(
-            src_ref=send_ref.at[rows],
-            dst_ref=recv_ref.at[rows],
-            send_sem=send_sem.at[o],
-            recv_sem=recv_sem.at[o],
-            device_id={"dom": me + by},
-            device_id_type=MESH,
-        )
-
-    for o in (2, 3, 0, 1):
-        by = sign * peer_offsets[o]
-
-        @pl.when(exists(by))
-        def _():
-            copy(o, by).start()
-
+
+def face_copy(sign, o, send_ref, recv_ref, send_sem, recv_sem):
+    rows = pl.ds(o * (send_ref.shape[0] // 4), send_ref.shape[0] // 4)
+    return pltpu.make_async_remote_copy(
+        src_ref=send_ref.at[rows],
+        dst_ref=recv_ref.at[rows],
+        send_sem=send_sem.at[o],
+        recv_sem=recv_sem.at[o],
+        device_id={"dom": lax.axis_index("dom") + sign * peer_offsets[o]},
+        device_id_type=MESH,
+    )
+
+
+def start_face(sign, o, *refs):
+    @pl.when(exists(sign * peer_offsets[o]))
+    def _():
+        face_copy(sign, o, *refs).start()
+
+
+def end_faces(sign, *refs):
+    recv_ref = refs[1]
+    slot = recv_ref.shape[0] // 4
     for o in range(4):
-        by = sign * peer_offsets[o]
-
-        @pl.when(jnp.logical_not(exists(-by)))
+
+        @pl.when(jnp.logical_not(exists(-sign * peer_offsets[o])))
         def _():
             recv_ref[pl.ds(o * slot, slot), :] = jnp.zeros(
                 (slot, recv_ref.shape[1]), recv_ref.dtype
             )
 
     for o in range(4):
-        by = sign * peer_offsets[o]
-
-        @pl.when(exists(by))
+
+        @pl.when(exists(sign * peer_offsets[o]))
         def _():
-            copy(o, by).wait_send()
-
-        @pl.when(exists(-by))
+            face_copy(sign, o, *refs).wait_send()
+
+        @pl.when(exists(-sign * peer_offsets[o]))
         def _():
-            copy(o, by).wait_recv()
-
-
-def exchange(values, sign):
+            face_copy(sign, o, *refs).wait_recv()
+
+
+def back_kernel(send_ref, recv_ref, send_sem, recv_sem):
+    refs = (send_ref, recv_ref, send_sem, recv_sem)
+    barrier = pltpu.get_barrier_semaphore()
+    greet_neighbours(barrier)
+    await_neighbours(barrier)
+    for o in (2, 3, 0, 1):
+        start_face(-1, o, *refs)
+    end_faces(-1, *refs)
+
+
+def exchange_back(values):
     return pl.pallas_call(
-        functools.partial(exchange_kernel, sign),
+        back_kernel,
         out_shape=jax.ShapeDtypeStruct(values.shape, values.dtype),
         in_specs=[VM],
         out_specs=VM,
         scratch_shapes=[pltpu.SemaphoreType.DMA((4,)), pltpu.SemaphoreType.DMA((4,))],
-        compiler_params=params(collective_id=1 if sign > 0 else 2, has_side_effects=True),
-        name="exchange_out" if sign > 0 else "exchange_back",
+        compiler_params=params(collective_id=2, has_side_effects=True),
+        name="exchange_back",
     )(values)
 
 
-def gather_faces(wide, targets_ref, stage, out_ref):
+def out_kernel(v_ref, targets_ref, recv_ref, wide, stage, send, send_sem, recv_sem):
+    nodes, columns = v_ref.shape
+    slot = send.shape[0] // 4
     group = 16
-
-    def step(i, carry):
-        base = pl.multiple_of(i * group, group)
-        rows = [wide[pl.ds(targets_ref[base + u], 1), :] for u in range(group)]
-        for u in range(group):
-            stage[pl.ds(base + u, 1), :] = rows[u]
-        return carry
-
-    lax.fori_loop(0, stage.shape[0] // group, step, 0)
-
-    def cast(rows):
-        out_ref[rows, :] = stage[rows, :].astype(out_ref.dtype)
-
-    chunks(stage.shape[0], 128, cast)
-
-
-def faces_kernel(v_ref, targets_ref, out_ref, wide, stage):
-    nodes = v_ref.shape[0]
+    refs = (send, recv_ref, send_sem, recv_sem)
+    barrier = pltpu.get_barrier_semaphore()
+    greet_neighbours(barrier)
 
     def widen(rows):
         wide[rows, :] = v_ref[rows, :].astype(jnp.float32)
 
     chunks(nodes, 256, widen)
-    wide[pl.ds(nodes, 8), :] = jnp.zeros((8, wide.shape[1]), jnp.float32)
-    gather_faces(wide, targets_ref, stage, out_ref)
-
-
-def faces_of(v, targets):
+    wide[pl.ds(nodes, 8), :] = jnp.zeros((8, columns), jnp.float32)
+    order = (0, 1, 2, 3)
+    for o in order:
+
+        def step(i, carry):
+            base = pl.multiple_of(o * slot + i * group, group)
+            rows = [wide[pl.ds(targets_ref[base + u], 1), :] for u in range(group)]
+            for u in range(group):
+                stage[pl.ds(base + u, 1), :] = rows[u]
+            return carry
+
+        lax.fori_loop(0, slot // group, step, 0)
+        rows = pl.ds(o * slot, slot)
+        send[rows, :] = stage[rows, :].astype(send.dtype)
+        if o == order[0]:
+            await_neighbours(barrier)
+        start_face(1, o, *refs)
+    end_faces(1, *refs)
+
+
+def exchange_out(v, targets):
     nodes, columns = v.shape
     count = targets.shape[0]
     return pl.pallas_call(
-        faces_kernel,
+        out_kernel,
         out_shape=jax.ShapeDtypeStruct((count, columns), v.dtype),
         in_specs=[VM, SM],
         out_specs=VM,
         scratch_shapes=[
             pltpu.VMEM((nodes + 8, columns), jnp.float32),
             pltpu.VMEM((count, columns), jnp.float32),
+            pltpu.VMEM((count, columns), v.dtype),
+            pltpu.SemaphoreType.DMA((4,)),
+            pltpu.SemaphoreType.DMA((4,)),
         ],
-        compiler_params=params(),
-        name="faces",
+        compiler_params=params(collective_id=1, has_side_effects=True),
+        name="exchange_out",
     )(v, targets)
 
 
@@ -265,11 +282,7 @@
     nodes, columns = v_ref.shape
     count = back_ref.shape[0]
     slot = count // 4
-    if first:
-        out_ref, faces_ref, wide, stage = rest[:4]
-    else:
-        out_ref = rest[0]
-    accs = rest[-4:]
+    out_ref, accs = rest[0], rest[1:]
     group = 4
 
     def fill(rows):
@@ -298,33 +311,21 @@
         image = total * coef + diag_ref[rows, :] * v_ref[rows, :].astype(jnp.float32)
         if first:
             value = image.astype(jnp.bfloat16)
-            wide[rows, :] = value.astype(jnp.float32)
         else:
             value = (2.0 * image - w_ref[rows, :].astype(jnp.float32)).astype(jnp.bfloat16)
         out_ref[rows, :] = value
 
     chunks(nodes, 64, finish)
-    if first:
-        wide[pl.ds(nodes, 8), :] = jnp.zeros((8, columns), jnp.float32)
-        gather_faces(wide, targets_ref, stage, faces_ref)
 
 
 def combine(first, own, back, v, w, diag, targets, coef):
     nodes, columns = v.shape
-    count = back.shape[0]
-    value = jax.ShapeDtypeStruct((nodes, columns), jnp.bfloat16)
-    faces = jax.ShapeDtypeStruct((count, columns), jnp.bfloat16)
-    extra = [
-        pltpu.VMEM((nodes + 8, columns), jnp.float32),
-        pltpu.VMEM((count, columns), jnp.float32),
-    ]
     return pl.pallas_call(
         functools.partial(combine_kernel, first),
-        out_shape=(value, faces) if first else value,
+        out_shape=jax.ShapeDtypeStruct((nodes, columns), jnp.bfloat16),
         in_specs=[VM, VM, VM, VM, VM, SM, SM],
-        out_specs=(VM, VM) if first else VM,
-        scratch_shapes=(extra if first else [])
-        + [pltpu.VMEM((nodes + 8, columns), jnp.float32)] * 4,
+        out_specs=VM,
+        scratch_shapes=[pltpu.VMEM((nodes + 8, columns), jnp.float32)] * 4,
         compiler_params=params(),
         name="combine_one" if first else "combine_two",
     )(own, back, v, w, diag, targets, coef)
@@ -428,37 +429,70 @@
 BLOCK = 64
 
 
-def inverse_factor(block):
-    lane = lax.broadcasted_iota(jnp.int32, (8, 2 * BLOCK), 1)
-    sub = lax.broadcasted_iota(jnp.int32, (8, 2 * BLOCK), 0)
+def inverse_factor(block, spread):
+    width = 2 * BLOCK
+    shape = (8, width)
+    count = BLOCK // 8
+    lane = lax.broadcasted_iota(jnp.int32, shape, 1)
+    sub = lax.broadcasted_iota(jnp.int32, shape, 0)
     doubled = jnp.concatenate([block, block], 1)
     tiles = []
-    for t in range(BLOCK // 8):
+    for t in range(count):
         unit = (lane - BLOCK == sub + 8 * t).astype(jnp.float32)
         tiles.append(jnp.where(lane < BLOCK, doubled[8 * t : 8 * t + 8], unit))
-    for j in range(BLOCK):
-        t, u = divmod(j, 8)
-        columns = {i: jnp.broadcast_to(tiles[i][:, j : j + 1], (8, 2 * BLOCK)) for i in range(t, BLOCK // 8)}
-        pivot = jnp.broadcast_to(columns[t][u : u + 1], (8, 2 * BLOCK))
-        row = jnp.broadcast_to(tiles[t][u : u + 1], (8, 2 * BLOCK)) / pivot
-        tiles[t] = tiles[t] - jnp.where(sub > u, columns[t], 0.0) * row
-        for i in range(t + 1, BLOCK // 8):
-            tiles[i] = tiles[i] - columns[i] * row
-    scaled = []
-    for t, tile in enumerate(tiles):
-        diagonal = jnp.sum(jnp.where(lane == sub + 8 * t, tile, 0.0), 1, keepdims=True)
-        scaled.append(tile * lax.rsqrt(diagonal))
-    return jnp.concatenate(scaled, 0)[:, BLOCK:]
-
-
-def finish_kernel(margin_ref, x_ref, other_ref, mine_ref, out_ref, work):
+    done = []
+    for g in range(count):
+        here = spread.at[g % 2]
+        for k in range(8):
+            here[8 * k : 8 * k + 8, :] = jnp.broadcast_to(tiles[g][:, 8 * g + k : 8 * g + k + 1], shape)
+        here[64:72, :] = tiles[g]
+
+        def replicated(at):
+            return jnp.broadcast_to(here[at : at + 1, :], shape)
+
+        a = [[replicated(8 * k + i) for k in range(i + 1)] for i in range(8)]
+        rows = [replicated(64 + i) for i in range(8)]
+        recip = []
+        for k in range(8):
+            recip.append(1.0 / a[k][k])
+            scaled = {i: a[i][k] * recip[k] for i in range(k + 1, 8)}
+            for i in range(k + 1, 8):
+                for l in range(k + 1, i + 1):
+                    a[i][l] = a[i][l] - scaled[i] * a[l][k]
+            for i in range(k + 1, 8):
+                rows[i] = rows[i] - scaled[i] * rows[k]
+                a[i][k] = scaled[i]
+        whole = rows[0] * lax.rsqrt(a[0][0])
+        for i in range(1, 8):
+            whole = jnp.where(sub == i, rows[i] * lax.rsqrt(a[i][i]), whole)
+        done.append(whole)
+        if g + 1 == count:
+            break
+        solved = [None] * 8
+        for i in range(7, -1, -1):
+            value = rows[i] * recip[i]
+            for l in range(7, i, -1):
+                value = value - a[l][i] * solved[l]
+            solved[i] = value
+        for t in range(g + 1, count):
+            parts = [
+                jnp.broadcast_to(tiles[t][:, 8 * g + k : 8 * g + k + 1], shape) * solved[k]
+                for k in range(8)
+            ]
+            while len(parts) > 1:
+                parts = [parts[n] + parts[n + 1] for n in range(0, len(parts), 2)]
+            tiles[t] = tiles[t] - parts[0]
+    return jnp.concatenate(done, 0)[:, BLOCK:]
+
+
+def finish_kernel(margin_ref, x_ref, other_ref, mine_ref, out_ref, work, spread):
     nodes, columns = x_ref.shape
     bands = margin_ref.shape[0]
     exact = lax.Precision.HIGHEST
     work[...] = margin_ref[...]
     for first in range(0, bands, BLOCK):
         last = first + BLOCK
-        inverse = inverse_factor(work[first:last, first:last])
+        inverse = inverse_factor(work[first:last, first:last], spread)
         pieces = [inverse]
         if first:
             pieces = [work[first:last, :first]] + pieces
@@ -502,7 +536,10 @@
         out_shape=jax.ShapeDtypeStruct(x.shape, jnp.float32),
         in_specs=[VM, VM, VM, SM],
         out_specs=VM,
-        scratch_shapes=[pltpu.VMEM(margin.shape, jnp.float32)],
+        scratch_shapes=[
+            pltpu.VMEM(margin.shape, jnp.float32),
+            pltpu.VMEM((2, 72, 2 * BLOCK), jnp.float32),
+        ],
         compiler_params=params(),
         name="finish",
     )(margin, x, other, mine)
@@ -517,14 +554,14 @@
     diag = jnp.broadcast_to(((potential - center) * coef)[:, None], (nodes, columns))
     coef = coef.reshape(1)
 
-    def apply_sums(vectors, faces):
-        ghosts = exchange(faces, 1)
+    def apply_sums(vectors):
+        ghosts = exchange_out(vectors, targets)
         own, back = operate(vectors, ghosts, cell_matrix, maps, cell_scale)
-        return own, exchange(back, -1)
-
-    own, back = apply_sums(wavefunctions, faces_of(wavefunctions, targets))
-    one, faces = combine(True, own, back, wavefunctions, wavefunctions, diag, targets, coef)
-    own, back = apply_sums(one, faces)
+        return own, exchange_back(back)
+
+    own, back = apply_sums(wavefunctions)
+    one = combine(True, own, back, wavefunctions, wavefunctions, diag, targets, coef)
+    own, back = apply_sums(one)
     two = combine(False, own, back, one, wavefunctions, diag, targets, coef)
     other, margin = margin_of(two, 1.0 / (nodes * lax.axis_size("dom")))
     return finish(margin, two, other, lax.axis_index("band").reshape(1))

time: 163 us -> 137 us (0.84)
  Pallas kernels: 156 us -> 129 us
    pallas_call x1, Pallas kernels: 39.9 us -> 14 us  [finish(): pl.pallas_call(finish_kernel, out_shape=jax.ShapeDtypeStruct(x.shape, jnp...]
    pallas_call x7 -> x6, Pallas kernels: 43.1 us -> 41.8 us  [the longest x2 17.2 us: exchange_out(): pl.pallas_call(out_kernel, out_shape=jax.ShapeDtypeStruct((count, columns...]
where the time goes in v3:
time: 137 us; the launch traced here: 136 us
  Pallas kernels  129 us (94%)
  local copies, waits for them, and re-layouts  3.43 us (3%)
  between operations  2.8 us (2%)
    pallas_call x2, Pallas kernels, operate(): pl.pallas_call(operate_kernel, out_shape=(jax.ShapeDtypeStruct((nodes, co...  50.6 us
    pallas_call x1, Pallas kernels, margin_of(): pl.pallas_call(functools.partial(margin_kernel, scaling), out_shape=(jax....  23.1 us
    pallas_call x2, Pallas kernels, exchange_out(): pl.pallas_call(out_kernel, out_shape=jax.ShapeDtypeStruct((count, columns...  17.2 us
    pallas_call x1, Pallas kernels, finish(): pl.pallas_call(finish_kernel, out_shape=jax.ShapeDtypeStruct(x.shape, jnp...  14 us
    pallas_call x2, Pallas kernels, exchange_back(): pl.pallas_call(back_kernel, out_shape=jax.ShapeDtypeStruct(values.shape,...  12.8 us
    pallas_call x2, Pallas kernels, combine(): pl.pallas_call(functools.partial(combine_kernel, first), out_shape=jax.Sh...  11.9 us

profile of v3, /device:TPU:0, one launch (start us, length us, event | category | flops | bytes accessed | tf_op | source)
XLA Modules:
  0.0 136.4 jit_solution(4182968243612065700)
XLA Ops:
  0.0 0.0 copy-start.4
  0.0 0.0 copy-start
  0.0 0.0 copy-start.3
  0.0 0.0 copy-start.2
  0.0 0.0 copy-start.1
  0.0 1.4 %fusion.1 = (f32[1]{0:T(128)}, f32[1]{0:T(128)}) fusion(f32[2]{0:T(128)} %param.8), kind=kLoop, calls=%fused_computation.3 | loop fusion | bytes 16 | tf_op jit(solution)/shard_map/slice | solution.py:552
  4.2 0.7 subtract_multiply_fusion
  4.9 2.0 %broadcast_in_dim.11.diag_ref = f32[4096,128]{1,0:T(8,128)} broadcast(f32[4096]{0:T(1024)S(1)} %subtract_multiply_fusion), dimensions={0} | broadcast | bytes 2113536 | tf_op jit(solution)/shard_map/broadcast_in_dim | solution.py:554
  6.8 0.0 copy-done.4
  6.8 0.0 copy-done
  6.9 8.9 %exchange_out.2.ghost_ref = bf16[1024,128]{1,0:T(8,128)(2,1)S(1)} custom-call(bf16[4096,128]{1,0:T(8,128)(2,1)S(1)} %copy-done, s32[1024]{0:T(1024)S(1)} %bitcast.10), custom_call_target="tpu_custom_call" | custom-call | tf_op jit(solution)/shard_map/exchange_out/pallas_call | solution.py:149
  15.7 0.0 copy-done.3
  15.8 0.0 copy-done.2
  15.8 0.0 copy-done.1
  15.8 25.3 %operate.2 = (f32[4096,128]{1,0:T(8,128)}, f32[1024,128]{1,0:T(8,128)S(1)}) custom-call(bf16[4096,128]{1,0:T(8,128)(2,1)S(1)} %copy-done, bf16[1024,128]{1,0:T(8,128)(2,1)S(1)} %exchange_out.2.ghost_ref, bf16[512,512]{1,0:T(8,128)(2,1)S(1)} %copy-done.1, s32[8192]{0:T(1024)S(1)} %bitcast.8, f32[16]{0:T(128)S(1)} %copy-done.2), custom_call_target="tpu_custom_call" | custom-call | tf_op jit(solution)/shard_map/operate/pallas_call | solution.py:263
  41.1 7.0 %exchange_back.2.back_ref = f32[1024,128]{1,0:T(8,128)S(1)} custom-call(f32[1024,128]{1,0:T(8,128)S(1)} %get-tuple-element.12.send_ref), custom_call_target="tpu_custom_call" | custom-call | tf_op jit(solution)/shard_map/exchange_back/pallas_call | solution.py:103
  48.1 5.8 %combine_one.1.v_ref = bf16[4096,128]{1,0:T(8,128)(2,1)S(1)} custom-call(f32[4096,128]{1,0:T(8,128)} %get-tuple-element.11.own_ref, f32[1024,128]{1,0:T(8,128)S(1)} %exchange_back.2.back_ref, bf16[4096,128]{1,0:T(8,128)(2,1)S(1)} %copy-done, bf16[4096,128]{1,0:T(8,128)(2,1)S(1)} %copy-done, f32[4096,128]{1,0:T(8,128)} %broadcast_in_dim.11.diag_ref, ...), custom_call_target="tpu_custom_call" | custom-call | tf_op jit(solution)/shard_map/combine_one/pallas_call | solution.py:323
  53.9 8.3 %exchange_out.3.ghost_ref = bf16[1024,128]{1,0:T(8,128)(2,1)S(1)} custom-call(bf16[4096,128]{1,0:T(8,128)(2,1)S(1)} %combine_one.1.v_ref, s32[1024]{0:T(1024)S(1)} %bitcast.12), custom_call_target="tpu_custom_call" | custom-call | tf_op jit(solution)/shard_map/exchange_out/pallas_call | solution.py:149
  62.2 25.3 %operate.3 = (f32[4096,128]{1,0:T(8,128)}, f32[1024,128]{1,0:T(8,128)S(1)}) custom-call(bf16[4096,128]{1,0:T(8,128)(2,1)S(1)} %combine_one.1.v_ref, bf16[1024,128]{1,0:T(8,128)(2,1)S(1)} %exchange_out.3.ghost_ref, bf16[512,512]{1,0:T(8,128)(2,1)S(1)} %copy-done.1, s32[8192]{0:T(1024)S(1)} %bitcast.9, f32[16]{0:T(128)S(1)} %copy-done.2), custom_call_target="tpu_custom_call" | custom-call | tf_op jit(solution)/shard_map/operate/pallas_call | solution.py:263
  87.5 5.8 %exchange_back.3.back_ref = f32[1024,128]{1,0:T(8,128)S(1)} custom-call(f32[1024,128]{1,0:T(8,128)S(1)} %get-tuple-element.14.send_ref), custom_call_target="tpu_custom_call" | custom-call | tf_op jit(solution)/shard_map/exchange_back/pallas_call | solution.py:103
  93.3 6.1 %combine_two.1.x_ref = bf16[4096,128]{1,0:T(8,128)(2,1)S(1)} custom-call(f32[4096,128]{1,0:T(8,128)} %get-tuple-element.13.own_ref, f32[1024,128]{1,0:T(8,128)S(1)} %exchange_back.3.back_ref, bf16[4096,128]{1,0:T(8,128)(2,1)S(1)} %combine_one.1.v_ref, bf16[4096,128]{1,0:T(8,128)(2,1)S(1)} %copy-done, f32[4096,128]{1,0:T(8,128)} %broadcast_in_dim.11.diag_ref, ...), custom_call_target="tpu_custom_call" | custom-call | tf_op jit(solution)/shard_map/combine_two/pallas_call | solution.py:323
  99.4 23.1 %margin.1 = (bf16[4096,128]{1,0:T(8,128)(2,1)S(1)}, f32[256,256]{1,0:T(8,128)S(1)}) custom-call(bf16[4096,128]{1,0:T(8,128)(2,1)S(1)} %combine_two.1.x_ref), custom_call_target="tpu_custom_call" | custom-call | tf_op jit(solution)/shard_map/margin/pallas_call | solution.py:410
  122.5 14.0 %finish.1 = f32[4096,128]{1,0:T(8,128)} custom-call(f32[256,256]{1,0:T(8,128)S(1)} %get-tuple-element.15.margin_ref, bf16[4096,128]{1,0:T(8,128)(2,1)S(1)} %combine_two.1.x_ref, bf16[4096,128]{1,0:T(8,128)(2,1)S(1)} %get-tuple-element.16.other_ref, s32[1]{0:T(128)} %bitcast.2.mine_ref), custom_call_target="tpu_custom_call" | custom-call | tf_op jit(solution)/shard_map/finish/pallas_call | solution.py:534
  (3 shorter events, 0.0 us)
Async XLA Ops:
  0.0 6.8 %copy-start.4 = (s32[4,256]{1,0:T(4,128)S(1)}, s32[4,256]{1,0:T(4,128)}, u32[]{:S(2)}) copy-start(s32[4,256]{1,0:T(4,128)} %param.13) | copy-start | bytes 12292
  0.0 6.8 %copy-start = (bf16[4096,128]{1,0:T(8,128)(2,1)S(1)}, bf16[4096,128]{1,0:T(8,128)(2,1)}, u32[]{:S(2)}) copy-start(bf16[4096,128]{1,0:T(8,128)(2,1)} %w_ref.3) | copy-start | bytes 3145732
  0.0 15.7 %copy-start.3 = (s32[16,512]{1,0:T(8,128)S(1)}, s32[16,512]{1,0:T(8,128)}, u32[]{:S(2)}) copy-start(s32[16,512]{1,0:T(8,128)} %param.12) | copy-start | bytes 98308
  0.0 15.7 %copy-start.2 = (f32[16]{0:T(128)S(1)}, f32[16]{0:T(128)}, u32[]{:S(2)}) copy-start(f32[16]{0:T(128)} %scale_ref.3) | copy-start | bytes 196
  0.0 15.8 %copy-start.1 = (bf16[512,512]{1,0:T(8,128)(2,1)S(1)}, bf16[512,512]{1,0:T(8,128)(2,1)}, u32[]{:S(2)}) copy-start(bf16[512,512]{1,0:T(8,128)(2,1)} %matrix_ref.3) | copy-start | bytes 1572868

commit v4 on v3

--- a/solution.py
+++ b/solution.py
@@ -14,8 +14,8 @@
 ACCS = 8
 
 
-def params(**more):
-    return pltpu.CompilerParams(vmem_limit_bytes=50 * 1024 * 1024, **more)
+def params(mib=20, **more):
+    return pltpu.CompilerParams(vmem_limit_bytes=mib * 1024 * 1024, **more)
 
 
 def chunks(total, size, body):
@@ -170,7 +170,7 @@
     ghosts = ghost_ref.shape[0]
     nc = matrix_ref.shape[0]
     cells = scale_ref.shape[0]
-    group = 8
+    group = 32
     gat, prod, accs = rest[:2], rest[2:4], rest[4:]
 
     def widen(rows):
@@ -191,28 +191,27 @@
     def gather_step(pair, base):
         rows = [
             (u, h, ext[pl.ds(maps_ref[(2 * pair + h) * nc + base + u], 1), :])
-            for u in range(group)
+            for u in range(ACCS // 2)
             for h in range(2)
         ]
         for u, h, row in rows:
             gat[h][pl.ds(base + u, 1), :] = row
 
     def scatter_step(pair, base):
-        for first in range(0, group, ACCS // 2):
-            spots = []
-            for u in range(ACCS // 2):
-                for h in range(2):
-                    at = pl.ds(maps_ref[(2 * pair + h) * nc + base + first + u], 1)
-                    acc = accs[2 * u + h]
-                    spots.append(
-                        (acc, at, acc[at, :] + prod[h][pl.ds(base + first + u, 1), :])
-                    )
-            for acc, at, value in spots:
-                acc[at, :] = value
+        spots = []
+        for u in range(ACCS // 2):
+            for h in range(2):
+                at = pl.ds(maps_ref[(2 * pair + h) * nc + base + u], 1)
+                acc = accs[2 * u + h]
+                spots.append((acc, at, acc[at, :] + prod[h][pl.ds(base + u, 1), :]))
+        for acc, at, value in spots:
+            acc[at, :] = value
 
     def rows_loop(body):
         def step(i, carry):
-            body(pl.multiple_of(i * group, group))
+            base = pl.multiple_of(i * group, group)
+            for first in range(0, group, ACCS // 2):
+                body(base + first)
             return carry
 
         lax.fori_loop(0, nc // group, step, 0)
@@ -273,12 +272,12 @@
         ]
         + [pltpu.VMEM((nc, columns), jnp.float32)] * 4
         + [pltpu.VMEM((nodes + count, columns), jnp.float32)] * ACCS,
-        compiler_params=params(),
+        compiler_params=params(36),
         name="operate",
     )(v, ghosts, matrix, maps, scale)
 
 
-def combine_kernel(first, own_ref, back_ref, v_ref, w_ref, diag_ref, targets_ref, coef_ref, *rest):
+def combine_kernel(first, own_ref, back_ref, v_ref, w_ref, potential_ref, targets_ref, bounds_ref, *rest):
     nodes, columns = v_ref.shape
     count = back_ref.shape[0]
     slot = count // 4
@@ -304,21 +303,21 @@
         return carry
 
     lax.fori_loop(0, slot // group, step, 0)
-    coef = coef_ref[0]
-
-    def finish(rows):
+    center = (bounds_ref[0] + bounds_ref[1]) * 0.5
+    coef = 1.0 / jnp.full((1, columns), (bounds_ref[1] - bounds_ref[0]) * 0.5, jnp.float32)
+    size = potential_ref.shape[1]
+    turned = potential_ref[...].T - center
+    for i in range(nodes // size):
+        rows = pl.ds(i * size, size)
         total = (accs[0][rows, :] + accs[1][rows, :]) + (accs[2][rows, :] + accs[3][rows, :])
-        image = total * coef + diag_ref[rows, :] * v_ref[rows, :].astype(jnp.float32)
-        if first:
-            value = image.astype(jnp.bfloat16)
-        else:
-            value = (2.0 * image - w_ref[rows, :].astype(jnp.float32)).astype(jnp.bfloat16)
-        out_ref[rows, :] = value
-
-    chunks(nodes, 64, finish)
-
-
-def combine(first, own, back, v, w, diag, targets, coef):
+        level = jnp.broadcast_to(turned[:, i : i + 1], (size, columns))
+        image = (total + level * v_ref[rows, :].astype(jnp.float32)) * coef
+        if not first:
+            image = 2.0 * image - w_ref[rows, :].astype(jnp.float32)
+        out_ref[rows, :] = image.astype(jnp.bfloat16)
+
+
+def combine(first, own, back, v, w, potential, targets, bounds):
     nodes, columns = v.shape
     return pl.pallas_call(
         functools.partial(combine_kernel, first),
@@ -328,85 +327,116 @@
         scratch_shapes=[pltpu.VMEM((nodes + 8, columns), jnp.float32)] * 4,
         compiler_params=params(),
         name="combine_one" if first else "combine_two",
-    )(own, back, v, w, diag, targets, coef)
+    )(own, back, v, w, potential, targets, bounds)
+
+
+PIECES = 4
 
 
 def margin_kernel(scaling, x_ref, other_ref, margin_ref, part, slots, send_sem, recv_sem):
-    columns = x_ref.shape[1]
-    nodes = x_ref.shape[0]
-    half_rows = columns // 2
+    nodes, columns = x_ref.shape
     me = lax.axis_index("dom")
     mine = lax.axis_index("band")
     size = lax.axis_size("dom")
-    bits = size.bit_length() - 1
-    partners = [{"band": 1 - mine}]
-    for k in range(bits):
-        bit = 1 << k
-        partners.append({"dom": me + bit - 2 * bit * (lax.div(me, bit) % 2)})
+    across = {"band": 1 - mine}
+    direct = columns // size >= 8
+    if direct:
+        peers = [{"dom": lax.rem(me + by, size)} for by in range(1, size)]
+    else:
+        peers = []
+        for k in range(size.bit_length() - 1):
+            bit = 1 << k
+            peers.append({"dom": me + bit - 2 * bit * (lax.div(me, bit) % 2)})
 
     barrier = pltpu.get_barrier_semaphore()
-    for partner in partners:
-        pl.semaphore_signal(barrier, inc=1, device_id=partner, device_id_type=MESH)
-    pl.semaphore_wait(barrier, len(partners))
-
-    def send(at, src, dst, partner):
+    for peer in [across] + peers:
+        pl.semaphore_signal(barrier, inc=1, device_id=peer, device_id_type=MESH)
+    pl.semaphore_wait(barrier, 1 + len(peers))
+
+    def send(at, src, dst, peer):
         copy = pltpu.make_async_remote_copy(
             src_ref=src,
             dst_ref=dst,
             send_sem=send_sem.at[at],
             recv_sem=recv_sem.at[at],
-            device_id=partner,
+            device_id=peer,
             device_id_type=MESH,
         )
         copy.start()
         return copy
 
-    panel = send(0, x_ref, other_ref, partners[0])
-    size_k = 512
-
-    def product(right, lanes):
+    chunk = nodes // PIECES
+    copies = []
+    for c in range(PIECES):
+        rows = pl.ds(c * chunk, chunk)
+        copies.append(send(c, x_ref.at[rows], other_ref.at[rows], across))
+    sums = jnp.zeros((columns, 2 * columns), jnp.float32)
+    for c in range(PIECES):
+        copies[c].wait()
+
         def step(i, total):
-            rows = pl.ds(pl.multiple_of(i * size_k, size_k), size_k)
+            rows = pl.ds(pl.multiple_of(c * chunk + i * 256, 256), 256)
+            own = x_ref[rows, :]
             return total + lax.dot_general(
-                x_ref[rows, :],
-                right[rows, :],
+                own,
+                jnp.concatenate([own, other_ref[rows, :]], 1),
                 (((0,), (0,)), ((), ())),
                 preferred_element_type=jnp.float32,
             )
 
-        part[:, lanes] = lax.fori_loop(
-            0, nodes // size_k, step, jnp.zeros((columns, columns), jnp.float32)
-        )
-
-    product(x_ref, pl.ds(0, columns))
-    panel.wait()
-    product(other_ref, pl.ds(columns, columns))
-
-    low = me % 2
-    keep = pl.ds(pl.multiple_of(low * half_rows, half_rows), half_rows)
-    give = pl.ds(pl.multiple_of((1 - low) * half_rows, half_rows), half_rows)
-    copy = send(1, part.at[give], slots.at[0], partners[1])
-    copy.wait()
-    part[keep, :] += slots[0]
-    for k in range(1, bits):
-        copy = send(1 + k, part.at[keep], slots.at[k], partners[1 + k])
-        copy.wait()
-        part[keep, :] += slots[k]
-    copy = send(1 + bits, part.at[keep], slots.at[bits], partners[1])
-    copy.wait()
-    part[give, :] = slots[bits]
-    rows_mine = pl.ds(pl.multiple_of(mine * columns, columns), columns)
+        sums = lax.fori_loop(0, chunk // 256, step, sums)
+    sums = sums * scaling
+    lanes_mine = pl.ds(pl.multiple_of(mine * columns, columns), columns)
     lanes_other = pl.ds(pl.multiple_of((1 - mine) * columns, columns), columns)
-    margin_ref[rows_mine, rows_mine] = part[:, :columns] * scaling
-    margin_ref[rows_mine, lanes_other] = part[:, columns:] * scaling
-    copy = send(2 + bits, margin_ref.at[rows_mine], margin_ref.at[rows_mine], partners[0])
-    copy.wait()
+    part[:, lanes_mine] = sums[:, :columns]
+    part[:, lanes_other] = sums[:, columns:]
+    at = PIECES
+
+    if direct:
+        piece = columns // size
+
+        def rows_of(owner):
+            return pl.ds(pl.multiple_of(owner * piece, piece), piece)
+
+        def margin_rows(owner):
+            return pl.ds(pl.multiple_of(mine * columns + owner * piece, piece), piece)
+
+        copies = []
+        for by in range(1, size):
+            to = lax.rem(me + by, size)
+            copies.append(send(at + by, part.at[rows_of(to)], slots.at[by], peers[by - 1]))
+        total = part[rows_of(me), :]
+        for by in range(1, size):
+            copies[by - 1].wait()
+            total = total + slots[by]
+        margin_ref[margin_rows(me), :] = total
+        at = at + size
+        home = margin_ref.at[margin_rows(me)]
+        copies = [send(at + by, home, home, peers[by - 1]) for by in range(1, size)]
+        at = at + size
+        forwards = [send(at, home, home, across)]
+        for by in range(1, size):
+            copies[by - 1].wait()
+            came = margin_ref.at[margin_rows(lax.rem(me + size - by, size))]
+            forwards.append(send(at + by, came, came, across))
+        for copy in forwards:
+            copy.wait()
+    else:
+        for k, peer in enumerate(peers):
+            copy = send(at + k, part, slots.at[k], peer)
+            copy.wait()
+            part[...] += slots[k]
+        margin_ref[lanes_mine, :] = part[...]
+        home = margin_ref.at[lanes_mine]
+        send(at + len(peers), home, home, across).wait()
 
 
 def margin_of(x, scaling):
     nodes, columns = x.shape
     size = lax.axis_size("dom")
-    bits = size.bit_length() - 1
+    direct = columns // size >= 8
+    slots = (size, columns // size) if direct else (size.bit_length(), columns)
+    copies = PIECES + (3 * size if direct else size.bit_length() + 1)
     return pl.pallas_call(
         functools.partial(margin_kernel, scaling),
         out_shape=(
@@ -417,9 +447,9 @@
         out_specs=(VM, VM),
         scratch_shapes=[
             pltpu.VMEM((columns, 2 * columns), jnp.float32),
-            pltpu.VMEM((bits + 1, columns // 2, 2 * columns), jnp.float32),
-            pltpu.SemaphoreType.DMA((bits + 3,)),
-            pltpu.SemaphoreType.DMA((bits + 3,)),
+            pltpu.VMEM(slots + (2 * columns,), jnp.float32),
+            pltpu.SemaphoreType.DMA((copies,)),
+            pltpu.SemaphoreType.DMA((copies,)),
         ],
         compiler_params=params(collective_id=3, has_side_effects=True),
         name="margin",
@@ -549,10 +579,7 @@
     nodes, columns = wavefunctions.shape
     targets = jnp.where(face_nodes >= 0, face_nodes, nodes).reshape(-1)
     maps = cell_nodes.reshape(-1)
-    center = (bounds[0] + bounds[1]) / 2.0
-    coef = 1.0 / ((bounds[1] - bounds[0]) / 2.0)
-    diag = jnp.broadcast_to(((potential - center) * coef)[:, None], (nodes, columns))
-    coef = coef.reshape(1)
+    levels = potential.reshape(nodes // 128, 128)
 
     def apply_sums(vectors):
         ghosts = exchange_out(vectors, targets)
@@ -560,9 +587,9 @@
         return own, exchange_back(back)
 
     own, back = apply_sums(wavefunctions)
-    one = combine(True, own, back, wavefunctions, wavefunctions, diag, targets, coef)
+    one = combine(True, own, back, wavefunctions, wavefunctions, levels, targets, bounds)
     own, back = apply_sums(one)
-    two = combine(False, own, back, one, wavefunctions, diag, targets, coef)
+    two = combine(False, own, back, one, wavefunctions, levels, targets, bounds)
     other, margin = margin_of(two, 1.0 / (nodes * lax.axis_size("dom")))
     return finish(margin, two, other, lax.axis_index("band").reshape(1))
 

time: 137 us -> 117 us (0.85)
  Pallas kernels: 129 us -> 112 us
  between operations: 2.8 us -> 0.13 us
    pallas_call x2, Pallas kernels: 50.6 us -> 41.4 us  [operate(): pl.pallas_call(operate_kernel, out_shape=(jax.ShapeDtypeStruct((nodes, co...]
    pallas_call x2, Pallas kernels: 11.9 us -> 7.84 us  [combine(): pl.pallas_call(functools.partial(combine_kernel, first), out_shape=jax.Sh...]
    pallas_call x1, Pallas kernels: 23.1 us -> 19.3 us  [margin_of(): pl.pallas_call(functools.partial(margin_kernel, scaling), out_shape=(jax....]
    unnamed x12 -> x16, local copies, waits for them, and re-layouts: 0.03 us -> 3.71 us
    broadcast_in_dim x1 -> x0, local copies, waits for them, and re-layouts: 1.95 us -> none  [on_device(): jnp.broadcast_to(((potential - center) * coef)[:, None], (nodes, columns))]
    slice x1 -> x0, local copies, waits for them, and re-layouts: 1.44 us -> none  [on_device(): center = (bounds[0] + bounds[1]) / 2.0]
where the time goes in v4:
time: 117 us
  Pallas kernels  112 us (96%)
  local copies, waits for them, and re-layouts  3.71 us (3%)
    pallas_call x2, Pallas kernels, operate(): pl.pallas_call(operate_kernel, out_shape=(jax.ShapeDtypeStruct((nodes, co...  41.4 us
    pallas_call x1, Pallas kernels, margin_of(): pl.pallas_call(functools.partial(margin_kernel, scaling), out_shape=(jax....  19.3 us
    pallas_call x2, Pallas kernels, exchange_out(): pl.pallas_call(out_kernel, out_shape=jax.ShapeDtypeStruct((count, columns...  17.1 us
    pallas_call x1, Pallas kernels, finish(): pl.pallas_call(finish_kernel, out_shape=jax.ShapeDtypeStruct(x.shape, jnp...  14 us
    pallas_call x2, Pallas kernels, exchange_back(): pl.pallas_call(back_kernel, out_shape=jax.ShapeDtypeStruct(values.shape,...  12.9 us
    pallas_call x2, Pallas kernels, combine(): pl.pallas_call(functools.partial(combine_kernel, first), out_shape=jax.Sh...  7.84 us
    unnamed x16, local copies, waits for them, and re-layouts  3.71 us

profile of v4, /device:TPU:0, one launch (start us, length us, event | category | flops | bytes accessed | tf_op | source)
XLA Modules:
  0.0 117.0 jit_solution(11392923249633915646)
XLA Ops:
  0.0 0.7 fusion
  0.7 0.0 copy-start
  0.7 1.2 %copy-done = bf16[4096,128]{1,0:T(8,128)(2,1)S(1)} copy-done((bf16[4096,128]{1,0:T(8,128)(2,1)S(1)}, bf16[4096,128]{1,0:T(8,128)(2,1)}, u32[]{:S(2)}) %copy-start) | copy-done | bytes 1048600
  1.9 0.0 copy-start.1
  1.9 0.0 copy-start.4
  1.9 0.0 copy-start.6
  1.9 8.8 %exchange_out.2.ghost_ref = bf16[1024,128]{1,0:T(8,128)(2,1)S(1)} custom-call(bf16[4096,128]{1,0:T(8,128)(2,1)S(1)} %copy-done, s32[1024]{0:T(1024)S(1)} %bitcast.9), custom_call_target="tpu_custom_call" | custom-call | tf_op jit(solution)/shard_map/exchange_out/pallas_call | solution.py:149
  10.8 0.8 copy.9
  11.5 0.0 copy-done.1
  11.5 0.0 copy-start.2
  11.6 1.0 copy-done.2
  12.6 0.0 copy-start.5
  12.6 0.7 copy-done.5
  13.2 20.7 %operate.2 = (f32[4096,128]{1,0:T(8,128)S(1)}, f32[1024,128]{1,0:T(8,128)S(1)}) custom-call(bf16[4096,128]{1,0:T(8,128)(2,1)S(1)} %copy-done.1, bf16[1024,128]{1,0:T(8,128)(2,1)S(1)} %exchange_out.2.ghost_ref, bf16[512,512]{1,0:T(8,128)(2,1)S(1)} %copy-done.2, s32[8192]{0:T(1024)S(1)} %bitcast.7, f32[16]{0:T(128)S(1)} %copy-done.5), custom_call_target="tpu_custom_call" | custom-call | tf_op jit(solution)/shard_map/operate/pallas_call | solution.py:262
  33.9 7.1 %exchange_back.2.back_ref = f32[1024,128]{1,0:T(8,128)S(1)} custom-call(f32[1024,128]{1,0:T(8,128)S(1)} %get-tuple-element.12.send_ref), custom_call_target="tpu_custom_call" | custom-call | tf_op jit(solution)/shard_map/exchange_back/pallas_call | solution.py:103
  41.0 0.0 copy-done.4
  41.0 0.0 copy-done.6
  41.1 0.0 copy-start.3
  41.1 3.8 %combine_one.1.v_ref = bf16[4096,128]{1,0:T(8,128)(2,1)S(1)} custom-call(f32[4096,128]{1,0:T(8,128)S(1)} %get-tuple-element.11.own_ref, f32[1024,128]{1,0:T(8,128)S(1)} %exchange_back.2.back_ref, bf16[4096,128]{1,0:T(8,128)(2,1)S(1)} %copy-done.1, bf16[4096,128]{1,0:T(8,128)(2,1)S(1)} %copy-done.1, f32[32,128]{1,0:T(8,128)S(1)} %bitcast.13, ...), custom_call_target="tpu_custom_call" | custom-call | tf_op jit(solution)/shard_map/combine_one/pallas_call | solution.py:322
  44.9 8.3 %exchange_out.3.ghost_ref = bf16[1024,128]{1,0:T(8,128)(2,1)S(1)} custom-call(bf16[4096,128]{1,0:T(8,128)(2,1)S(1)} %combine_one.1.v_ref, s32[1024]{0:T(1024)S(1)} %bitcast.11), custom_call_target="tpu_custom_call" | custom-call | tf_op jit(solution)/shard_map/exchange_out/pallas_call | solution.py:149
  53.1 0.0 copy-done.3
  53.1 20.7 %operate.3 = (f32[4096,128]{1,0:T(8,128)S(1)}, f32[1024,128]{1,0:T(8,128)S(1)}) custom-call(bf16[4096,128]{1,0:T(8,128)(2,1)S(1)} %combine_one.1.v_ref, bf16[1024,128]{1,0:T(8,128)(2,1)S(1)} %exchange_out.3.ghost_ref, bf16[512,512]{1,0:T(8,128)(2,1)S(1)} %copy-done.3, s32[8192]{0:T(1024)S(1)} %bitcast.8, f32[16]{0:T(128)S(1)} %copy-done.5), custom_call_target="tpu_custom_call" | custom-call | tf_op jit(solution)/shard_map/operate/pallas_call | solution.py:262
  73.8 5.8 %exchange_back.3.back_ref = f32[1024,128]{1,0:T(8,128)S(1)} custom-call(f32[1024,128]{1,0:T(8,128)S(1)} %get-tuple-element.14.send_ref), custom_call_target="tpu_custom_call" | custom-call | tf_op jit(solution)/shard_map/exchange_back/pallas_call | solution.py:103
  79.7 4.0 %combine_two.1.x_ref = bf16[4096,128]{1,0:T(8,128)(2,1)S(1)} custom-call(f32[4096,128]{1,0:T(8,128)S(1)} %get-tuple-element.13.own_ref, f32[1024,128]{1,0:T(8,128)S(1)} %exchange_back.3.back_ref, bf16[4096,128]{1,0:T(8,128)(2,1)S(1)} %combine_one.1.v_ref, bf16[4096,128]{1,0:T(8,128)(2,1)S(1)} %copy-done.1, f32[32,128]{1,0:T(8,128)S(1)} %bitcast.14, ...), custom_call_target="tpu_custom_call" | custom-call | tf_op jit(solution)/shard_map/combine_two/pallas_call | solution.py:322
  83.7 19.3 %margin.1 = (bf16[4096,128]{1,0:T(8,128)(2,1)S(1)}, f32[256,256]{1,0:T(8,128)S(1)}) custom-call(bf16[4096,128]{1,0:T(8,128)(2,1)S(1)} %combine_two.1.x_ref), custom_call_target="tpu_custom_call" | custom-call | tf_op jit(solution)/shard_map/margin/pallas_call | solution.py:440
  103.0 14.0 %finish.1 = f32[4096,128]{1,0:T(8,128)} custom-call(f32[256,256]{1,0:T(8,128)S(1)} %get-tuple-element.15.margin_ref, bf16[4096,128]{1,0:T(8,128)(2,1)S(1)} %combine_two.1.x_ref, bf16[4096,128]{1,0:T(8,128)(2,1)S(1)} %get-tuple-element.16.other_ref, s32[1]{0:T(128)} %bitcast.1.mine_ref), custom_call_target="tpu_custom_call" | custom-call | tf_op jit(solution)/shard_map/finish/pallas_call | solution.py:564
  (1 shorter events, 0.0 us)
Async XLA Ops:
  0.7 1.2 %copy-start = (bf16[4096,128]{1,0:T(8,128)(2,1)S(1)}, bf16[4096,128]{1,0:T(8,128)(2,1)}, u32[]{:S(2)}) copy-start(bf16[4096,128]{1,0:T(8,128)(2,1)} %w_ref.3) | copy-start | bytes 3145732
  1.9 9.6 %copy-start.1 = (bf16[4096,128]{1,0:T(8,128)(2,1)S(1)}, bf16[4096,128]{1,0:T(8,128)(2,1)}, u32[]{:S(2)}) copy-start(bf16[4096,128]{1,0:T(8,128)(2,1)} %w_ref.3) | copy-start | bytes 3145732
  1.9 39.1 %copy-start.4 = (f32[4096]{0:T(1024)S(1)}, f32[4096]{0:T(1024)}, u32[]{:S(2)}) copy-start(f32[4096]{0:T(1024)} %param.11) | copy-start | bytes 49156
  1.9 39.1 %copy-start.6 = (f32[2]{0:T(128)S(1)}, f32[2]{0:T(128)}, u32[]{:S(2)}) copy-start(f32[2]{0:T(128)} %bounds_ref.3) | copy-start | bytes 28
  11.5 1.0 copy-start.2
  12.6 0.7 copy-start.5
  41.1 12.1 %copy-start.3 = (bf16[512,512]{1,0:T(8,128)(2,1)S(1)}, bf16[512,512]{1,0:T(8,128)(2,1)}, u32[]{:S(2)}) copy-start(bf16[512,512]{1,0:T(8,128)(2,1)} %matrix_ref.3) | copy-start | bytes 1572868

commit v5 on v4

--- a/solution.py
+++ b/solution.py
@@ -170,8 +170,8 @@
     ghosts = ghost_ref.shape[0]
     nc = matrix_ref.shape[0]
     cells = scale_ref.shape[0]
-    group = 32
-    gat, prod, accs = rest[:2], rest[2:4], rest[4:]
+    group = 64
+    gat, prods, both, accs = rest[:2], (rest[2:4], rest[4:6]), rest[6], rest[7:]
 
     def widen(rows):
         ext[rows, :] = v_ref[rows, :].astype(jnp.float32)
@@ -198,6 +198,7 @@
             gat[h][pl.ds(base + u, 1), :] = row
 
     def scatter_step(pair, base):
+        prod = prods[pair % 2]
         spots = []
         for u in range(ACCS // 2):
             for h in range(2):
@@ -207,39 +208,35 @@
         for acc, at, value in spots:
             acc[at, :] = value
 
-    def rows_loop(body):
+    def multiply(pair, base):
+        rows = pl.ds(base, group)
+        result = jnp.dot(matrix_ref[rows, :], both[...], preferred_element_type=jnp.float32)
+        for h in range(2):
+            prods[pair % 2][h][rows, :] = (
+                result[:, h * columns : (h + 1) * columns] * scale_ref[2 * pair + h]
+            )
+
+    pairs = cells // 2
+    for stage in range(pairs + 2):
+        gathers = stage < pairs
+        multiplies = 0 <= stage - 1 < pairs
+        scatters = 0 <= stage - 2 < pairs
+        if multiplies:
+            for h in range(2):
+                both[:, h * columns : (h + 1) * columns] = gat[h][...].astype(both.dtype)
+
         def step(i, carry):
             base = pl.multiple_of(i * group, group)
+            if multiplies:
+                multiply(stage - 1, base)
             for first in range(0, group, ACCS // 2):
-                body(base + first)
+                if gathers:
+                    gather_step(stage, base + first)
+                if scatters:
+                    scatter_step(stage - 2, base + first)
             return carry
 
         lax.fori_loop(0, nc // group, step, 0)
-
-    def multiply(pair):
-        both = jnp.concatenate([gat[0][...], gat[1][...]], 1).astype(jnp.bfloat16)
-        result = jnp.dot(matrix_ref[...], both, preferred_element_type=jnp.float32)
-        for h in range(2):
-            prod[h][...] = (
-                result[:, h * columns : (h + 1) * columns] * scale_ref[2 * pair + h]
-            )
-
-    rows_loop(lambda base: gather_step(0, base))
-
-    def pair_step(pair, carry):
-        multiply(pair)
-
-        def both(base):
-            gather_step(pair + 1, base)
-            scatter_step(pair, base)
-
-        rows_loop(both)
-        return carry
-
-    last = cells // 2 - 1
-    lax.fori_loop(0, last, pair_step, 0)
-    multiply(last)
-    rows_loop(lambda base: scatter_step(last, base))
 
     def total(rows):
         value = accs[0][rows, :]
@@ -252,7 +249,9 @@
 
     chunks(nodes, 64, collect)
     for part in range(ghosts // 64):
-        back_ref[pl.ds(part * 64, 64), :] = total(pl.ds(nodes + part * 64, 64))
+        back_ref[pl.ds(part * 64, 64), :] = total(pl.ds(nodes + part * 64, 64)).astype(
+            back_ref.dtype
+        )
 
 
 def operate(v, ghosts, matrix, maps, scale):
@@ -270,7 +269,8 @@
         scratch_shapes=[
             pltpu.VMEM((nodes + count, columns), jnp.float32),
         ]
-        + [pltpu.VMEM((nc, columns), jnp.float32)] * 4
+        + [pltpu.VMEM((nc, columns), jnp.float32)] * 6
+        + [pltpu.VMEM((nc, 2 * columns), matrix.dtype)]
         + [pltpu.VMEM((nodes + count, columns), jnp.float32)] * ACCS,
         compiler_params=params(36),
         name="operate",
@@ -281,7 +281,8 @@
     nodes, columns = v_ref.shape
     count = back_ref.shape[0]
     slot = count // 4
-    out_ref, accs = rest[0], rest[1:]
+    out_ref, wide, accs = rest[0], rest[1], rest[2:]
+    wide[...] = back_ref[...].astype(jnp.float32)
     group = 4
 
     def fill(rows):
@@ -297,7 +298,7 @@
             for o in range(4):
                 row = i * group + u + o * slot
                 at = pl.ds(targets_ref[row], 1)
-                spots.append((accs[o], at, accs[o][at, :] + back_ref[pl.ds(row, 1), :]))
+                spots.append((accs[o], at, accs[o][at, :] + wide[pl.ds(row, 1), :]))
             for acc, at, value in spots:
                 acc[at, :] = value
         return carry
@@ -324,7 +325,8 @@
         out_shape=jax.ShapeDtypeStruct((nodes, columns), jnp.bfloat16),
         in_specs=[VM, VM, VM, VM, VM, SM, SM],
         out_specs=VM,
-        scratch_shapes=[pltpu.VMEM((nodes + 8, columns), jnp.float32)] * 4,
+        scratch_shapes=[pltpu.VMEM(back.shape, jnp.float32)]
+        + [pltpu.VMEM((nodes + 8, columns), jnp.float32)] * 4,
         compiler_params=params(),
         name="combine_one" if first else "combine_two",
     )(own, back, v, w, potential, targets, bounds)
@@ -373,18 +375,14 @@
     sums = jnp.zeros((columns, 2 * columns), jnp.float32)
     for c in range(PIECES):
         copies[c].wait()
-
-        def step(i, total):
-            rows = pl.ds(pl.multiple_of(c * chunk + i * 256, 256), 256)
-            own = x_ref[rows, :]
-            return total + lax.dot_general(
-                own,
-                jnp.concatenate([own, other_ref[rows, :]], 1),
-                (((0,), (0,)), ((), ())),
-                preferred_element_type=jnp.float32,
-            )
-
-        sums = lax.fori_loop(0, chunk // 256, step, sums)
+        rows = pl.ds(c * chunk, chunk)
+        own = x_ref[rows, :]
+        sums = sums + lax.dot_general(
+            own,
+            jnp.concatenate([own, other_ref[rows, :]], 1),
+            (((0,), (0,)), ((), ())),
+            preferred_element_type=jnp.float32,
+        )
     sums = sums * scaling
     lanes_mine = pl.ds(pl.multiple_of(mine * columns, columns), columns)
     lanes_other = pl.ds(pl.multiple_of((1 - mine) * columns, columns), columns)

time: 117 us -> 115 us (0.983)
  Pallas kernels: 112 us -> 110 us
    pallas_call x1, Pallas kernels: 19.3 us -> 17.5 us  [margin_of(): pl.pallas_call(functools.partial(margin_kernel, scaling), out_shape=(jax....]
where the time goes in v5:
time: 115 us
  Pallas kernels  110 us (96%)
  local copies, waits for them, and re-layouts  3.71 us (3%)
    pallas_call x2, Pallas kernels, operate(): pl.pallas_call(operate_kernel, out_shape=(jax.ShapeDtypeStruct((nodes, co...  40.7 us
    pallas_call x1, Pallas kernels, margin_of(): pl.pallas_call(functools.partial(margin_kernel, scaling), out_shape=(jax....  17.5 us
    pallas_call x2, Pallas kernels, exchange_out(): pl.pallas_call(out_kernel, out_shape=jax.ShapeDtypeStruct((count, columns...  17.1 us
    pallas_call x1, Pallas kernels, finish(): pl.pallas_call(finish_kernel, out_shape=jax.ShapeDtypeStruct(x.shape, jnp...  14 us
    pallas_call x2, Pallas kernels, exchange_back(): pl.pallas_call(back_kernel, out_shape=jax.ShapeDtypeStruct(values.shape,...  12.9 us
    pallas_call x2, Pallas kernels, combine(): pl.pallas_call(functools.partial(combine_kernel, first), out_shape=jax.Sh...  7.91 us
    unnamed x16, local copies, waits for them, and re-layouts  3.71 us

profile of v5, /device:TPU:0, one launch (start us, length us, event | category | flops | bytes accessed | tf_op | source)
XLA Modules:
  0.0 114.6 jit_solution(7845617855393185071)
XLA Ops:
  0.0 0.7 fusion
  0.7 0.0 copy-start
  0.7 1.2 %copy-done = bf16[4096,128]{1,0:T(8,128)(2,1)S(1)} copy-done((bf16[4096,128]{1,0:T(8,128)(2,1)S(1)}, bf16[4096,128]{1,0:T(8,128)(2,1)}, u32[]{:S(2)}) %copy-start) | copy-done | bytes 1048600
  1.9 0.0 copy-start.1
  1.9 0.0 copy-start.4
  1.9 0.0 copy-start.6
  1.9 8.8 %exchange_out.2.ghost_ref = bf16[1024,128]{1,0:T(8,128)(2,1)S(1)} custom-call(bf16[4096,128]{1,0:T(8,128)(2,1)S(1)} %copy-done, s32[1024]{0:T(1024)S(1)} %bitcast.9), custom_call_target="tpu_custom_call" | custom-call | tf_op jit(solution)/shard_map/exchange_out/pallas_call | solution.py:149
  10.8 0.8 copy.9
  11.5 0.0 copy-done.1
  11.5 0.0 copy-start.2
  11.6 1.0 copy-done.2
  12.6 0.0 copy-start.5
  12.6 0.7 copy-done.5
  13.2 20.3 %operate.2 = (f32[4096,128]{1,0:T(8,128)S(1)}, f32[1024,128]{1,0:T(8,128)S(1)}) custom-call(bf16[4096,128]{1,0:T(8,128)(2,1)S(1)} %copy-done.1, bf16[1024,128]{1,0:T(8,128)(2,1)S(1)} %exchange_out.2.ghost_ref, bf16[512,512]{1,0:T(8,128)(2,1)S(1)} %copy-done.2, s32[8192]{0:T(1024)S(1)} %bitcast.7, f32[16]{0:T(128)S(1)} %copy-done.5), custom_call_target="tpu_custom_call" | custom-call | tf_op jit(solution)/shard_map/operate/pallas_call | solution.py:261
  33.6 7.1 %exchange_back.2.back_ref = f32[1024,128]{1,0:T(8,128)S(1)} custom-call(f32[1024,128]{1,0:T(8,128)S(1)} %get-tuple-element.12.send_ref), custom_call_target="tpu_custom_call" | custom-call | tf_op jit(solution)/shard_map/exchange_back/pallas_call | solution.py:103
  40.7 0.0 copy-done.4
  40.7 0.0 copy-done.6
  40.7 0.0 copy-start.3
  40.7 3.8 %combine_one.1.v_ref = bf16[4096,128]{1,0:T(8,128)(2,1)S(1)} custom-call(f32[4096,128]{1,0:T(8,128)S(1)} %get-tuple-element.11.own_ref, f32[1024,128]{1,0:T(8,128)S(1)} %exchange_back.2.back_ref, bf16[4096,128]{1,0:T(8,128)(2,1)S(1)} %copy-done.1, bf16[4096,128]{1,0:T(8,128)(2,1)S(1)} %copy-done.1, f32[32,128]{1,0:T(8,128)S(1)} %bitcast.13, ...), custom_call_target="tpu_custom_call" | custom-call | tf_op jit(solution)/shard_map/combine_one/pallas_call | solution.py:323
  44.5 8.3 %exchange_out.3.ghost_ref = bf16[1024,128]{1,0:T(8,128)(2,1)S(1)} custom-call(bf16[4096,128]{1,0:T(8,128)(2,1)S(1)} %combine_one.1.v_ref, s32[1024]{0:T(1024)S(1)} %bitcast.11), custom_call_target="tpu_custom_call" | custom-call | tf_op jit(solution)/shard_map/exchange_out/pallas_call | solution.py:149
  52.8 0.0 copy-done.3
  52.8 20.3 %operate.3 = (f32[4096,128]{1,0:T(8,128)S(1)}, f32[1024,128]{1,0:T(8,128)S(1)}) custom-call(bf16[4096,128]{1,0:T(8,128)(2,1)S(1)} %combine_one.1.v_ref, bf16[1024,128]{1,0:T(8,128)(2,1)S(1)} %exchange_out.3.ghost_ref, bf16[512,512]{1,0:T(8,128)(2,1)S(1)} %copy-done.3, s32[8192]{0:T(1024)S(1)} %bitcast.8, f32[16]{0:T(128)S(1)} %copy-done.5), custom_call_target="tpu_custom_call" | custom-call | tf_op jit(solution)/shard_map/operate/pallas_call | solution.py:261
  73.2 5.8 %exchange_back.3.back_ref = f32[1024,128]{1,0:T(8,128)S(1)} custom-call(f32[1024,128]{1,0:T(8,128)S(1)} %get-tuple-element.14.send_ref), custom_call_target="tpu_custom_call" | custom-call | tf_op jit(solution)/shard_map/exchange_back/pallas_call | solution.py:103
  79.0 4.1 %combine_two.1.x_ref = bf16[4096,128]{1,0:T(8,128)(2,1)S(1)} custom-call(f32[4096,128]{1,0:T(8,128)S(1)} %get-tuple-element.13.own_ref, f32[1024,128]{1,0:T(8,128)S(1)} %exchange_back.3.back_ref, bf16[4096,128]{1,0:T(8,128)(2,1)S(1)} %combine_one.1.v_ref, bf16[4096,128]{1,0:T(8,128)(2,1)S(1)} %copy-done.1, f32[32,128]{1,0:T(8,128)S(1)} %bitcast.14, ...), custom_call_target="tpu_custom_call" | custom-call | tf_op jit(solution)/shard_map/combine_two/pallas_call | solution.py:323
  83.1 17.5 %margin.1 = (bf16[4096,128]{1,0:T(8,128)(2,1)S(1)}, f32[256,256]{1,0:T(8,128)S(1)}) custom-call(bf16[4096,128]{1,0:T(8,128)(2,1)S(1)} %combine_two.1.x_ref), custom_call_target="tpu_custom_call" | custom-call | tf_op jit(solution)/shard_map/margin/pallas_call | solution.py:438
  100.6 14.0 %finish.1 = f32[4096,128]{1,0:T(8,128)} custom-call(f32[256,256]{1,0:T(8,128)S(1)} %get-tuple-element.15.margin_ref, bf16[4096,128]{1,0:T(8,128)(2,1)S(1)} %combine_two.1.x_ref, bf16[4096,128]{1,0:T(8,128)(2,1)S(1)} %get-tuple-element.16.other_ref, s32[1]{0:T(128)} %bitcast.1.mine_ref), custom_call_target="tpu_custom_call" | custom-call | tf_op jit(solution)/shard_map/finish/pallas_call | solution.py:562
  (1 shorter events, 0.0 us)
Async XLA Ops:
  0.7 1.2 %copy-start = (bf16[4096,128]{1,0:T(8,128)(2,1)S(1)}, bf16[4096,128]{1,0:T(8,128)(2,1)}, u32[]{:S(2)}) copy-start(bf16[4096,128]{1,0:T(8,128)(2,1)} %w_ref.3) | copy-start | bytes 3145732
  1.9 9.6 %copy-start.1 = (bf16[4096,128]{1,0:T(8,128)(2,1)S(1)}, bf16[4096,128]{1,0:T(8,128)(2,1)}, u32[]{:S(2)}) copy-start(bf16[4096,128]{1,0:T(8,128)(2,1)} %w_ref.3) | copy-start | bytes 3145732
  1.9 38.8 %copy-start.4 = (f32[4096]{0:T(1024)S(1)}, f32[4096]{0:T(1024)}, u32[]{:S(2)}) copy-start(f32[4096]{0:T(1024)} %param.11) | copy-start | bytes 49156
  1.9 38.8 %copy-start.6 = (f32[2]{0:T(128)S(1)}, f32[2]{0:T(128)}, u32[]{:S(2)}) copy-start(f32[2]{0:T(128)} %bounds_ref.3) | copy-start | bytes 28
  11.5 1.0 copy-start.2
  12.6 0.7 copy-start.5
  40.7 12.1 %copy-start.3 = (bf16[512,512]{1,0:T(8,128)(2,1)S(1)}, bf16[512,512]{1,0:T(8,128)(2,1)}, u32[]{:S(2)}) copy-start(bf16[512,512]{1,0:T(8,128)(2,1)} %matrix_ref.3) | copy-start | bytes 1572868
